TPU v7x, 256 devices: a whole 4x4x8 slice. The times are simulated.
256 devices in a mesh: dp: 32 (over z, x_lo, core), ctx: 8 (over x_hi, y).
Axes of the slice: x: 4 (x_hi: 2, x_lo: 2; x = x_hi * 2 + x_lo), y: 4, z: 8, core: 2. Of those that a mesh axis runs over, the one named last changes fastest.
Arguments:
- tokens: bfloat16 [65536, 512], P(('dp', 'ctx')), may hold values from -24 to 24
- seq_lengths: int32 [32, 2], P('dp'), may hold values from 1 to 1920, 2048 in all within a row
- w_in: bfloat16 [512, 2048], P('dp'), may hold values from -0.25 to 0.25
- w_out: bfloat16 [512, 512], P('dp'), may hold values from -0.25 to 0.25
- cotangent: bfloat16 [65536, 512], P(('dp', 'ctx')), may hold values from -6 to 6
Outputs:
- layer_out: bfloat16 [65536, 512], P(('dp', 'ctx'))
- d_tokens: bfloat16 [65536, 512], P(('dp', 'ctx'))
- grad_in: float32 [512, 2048], P('dp')
- grad_out: float32 [512, 512], P('dp')
Inputs may be any that keep to these rules, and one draw needn't show every extreme that they name: `seq_lengths`: each row lists the lengths of the 2 sequences that fill one group of 2048 positions, in order of position, and sums to 2048; its largest entry is at most 1920.
All inputs are finite; a program needn't handle non-finite values.
Results may differ from a plain program's by a relative error of at most 0.0083.
Values may be sent and summed in bfloat16 or wider, within the bound.
A program may use at most 64 MiB of HBM per device.

v0:
```python
import math

import jax
import jax.numpy as jnp
from jax import lax
from jax.sharding import PartitionSpec as P

HEADS = 4


NORM_EPS = 1e-05


def shifted(shard, axis, by):
    count = lax.axis_size(axis)
    return lax.ppermute(shard, axis, [(i, (i + by) % count) for i in range(count)])


def norm_rows(values_in):
    centre = values_in - jnp.mean(values_in, axis=-1, keepdims=True)
    spread = lax.rsqrt(jnp.mean(centre * centre, axis=-1, keepdims=True) + NORM_EPS)
    return (centre * spread, spread)


def norm_back(gradient, normed, spread):
    first_mean = jnp.mean(gradient, axis=-1, keepdims=True)
    second_mean = jnp.mean(gradient * normed, axis=-1, keepdims=True)
    return spread * (gradient - first_mean - normed * second_mean)


def silu_slope(values_in):
    sigmoid_v = jax.nn.sigmoid(values_in)
    return sigmoid_v * (1.0 + values_in * (1.0 - sigmoid_v))


def stored_places(stored, block_rows, cycle_count):
    half_rows = block_rows // 2
    block_id = stored // block_rows
    offset = stored % block_rows
    early = block_id * half_rows + offset
    late = (2 * cycle_count - 1 - block_id) * half_rows + offset - half_rows
    return jnp.where(offset < half_rows, early, late)


def body(tokens, seq_lengths, w_in, w_out, cotangent):
    tok_rows = tokens.shape[0]
    model_width = tokens.shape[1]
    head_size = model_width // HEADS
    score_scale = 1.0 / math.sqrt(head_size)
    my_rank = lax.axis_index("ctx")
    cycle_size = lax.axis_size("ctx")
    seq_ends = jnp.cumsum(seq_lengths[0])
    own_start = my_rank * tok_rows

    def places_of(first_row, count):
        return stored_places(first_row + jnp.arange(count, dtype=jnp.int32), tok_rows, cycle_size)

    def labels_of(places):
        return jnp.sum((places[:, None] >= seq_ends[None, :]).astype(jnp.int32), axis=1)

    def allowed_of(query_start, query_count, key_start, key_count):
        query_places = places_of(query_start, query_count)
        key_places = places_of(key_start, key_count)
        same_label = labels_of(query_places)[:, None] == labels_of(key_places)[None, :]
        causal = key_places[None, :] <= query_places[:, None]
        return same_label & causal

    def split_heads(block):
        return block.reshape(block.shape[0], HEADS, head_size)

    def forward_block(query_rows, query_start, key_rows, value_rows, key_start):
        allowed = allowed_of(query_start, query_rows.shape[0], key_start, key_rows.shape[0])
        scores = score_scale * jnp.einsum(
            "ihd,jhd->hij",
            split_heads(query_rows),
            split_heads(key_rows),
            preferred_element_type=jnp.float32,
        )
        attn_weights = jnp.where(allowed[None], jax.nn.silu(scores), 0.0).astype(jnp.bfloat16)
        mixed_part = jnp.einsum(
            "hij,jhd->ihd",
            attn_weights,
            split_heads(value_rows),
            preferred_element_type=jnp.float32,
        )
        return mixed_part.reshape(query_rows.shape[0], model_width)

    def backward_block(query_rows, d_mixed_rows, query_start, key_rows, value_rows, key_start):
        allowed = allowed_of(query_start, query_rows.shape[0], key_start, key_rows.shape[0])
        query_heads = split_heads(query_rows)
        key_heads = split_heads(key_rows)
        d_mixed_heads = split_heads(d_mixed_rows)
        scores = score_scale * jnp.einsum(
            "ihd,jhd->hij", query_heads, key_heads, preferred_element_type=jnp.float32
        )
        attn_weights = jnp.where(allowed[None], jax.nn.silu(scores), 0.0).astype(jnp.bfloat16)
        d_value = jnp.einsum(
            "hij,ihd->jhd", attn_weights, d_mixed_heads, preferred_element_type=jnp.float32
        )
        d_attn = jnp.einsum(
            "ihd,jhd->hij",
            d_mixed_heads,
            split_heads(value_rows),
            preferred_element_type=jnp.float32,
        )
        d_scores = jnp.where(allowed[None], d_attn * silu_slope(scores), 0.0).astype(jnp.bfloat16)
        d_query = score_scale * jnp.einsum(
            "hij,jhd->ihd", d_scores, key_heads, preferred_element_type=jnp.float32
        )
        d_key = score_scale * jnp.einsum(
            "hij,ihd->jhd", d_scores, query_heads, preferred_element_type=jnp.float32
        )
        return (
            d_query.reshape(query_rows.shape[0], model_width),
            d_key.reshape(key_rows.shape[0], model_width),
            d_value.reshape(key_rows.shape[0], model_width),
        )

    x_float = tokens.astype(jnp.float32)
    x_normed, x_spread = norm_rows(x_float)
    x_normed_b = x_normed.astype(jnp.bfloat16)
    w_whole = lax.all_gather(w_in, "dp", axis=0, tiled=True)
    pre_act = jnp.dot(x_normed_b, w_whole, preferred_element_type=jnp.float32)
    projected = jax.nn.silu(pre_act).astype(jnp.bfloat16)
    gate_float = projected[:, :model_width].astype(jnp.float32)
    query_rows = projected[:, model_width : 2 * model_width]
    key_rows = projected[:, 2 * model_width : 3 * model_width]
    value_rows = projected[:, 3 * model_width :]
    first_mixed = forward_block(query_rows, own_start, key_rows, value_rows, own_start)

    def loop_step(step_index, state_now):
        key_pair, running = state_now
        key_pair = shifted(key_pair, "ctx", 1)
        source = jnp.mod(my_rank - step_index, cycle_size)
        return (
            key_pair,
            running
            + forward_block(query_rows, own_start, key_pair[0], key_pair[1], source * tok_rows),
        )

    unused_pair, mixed_sum = lax.fori_loop(
        1, cycle_size, loop_step, (jnp.stack([key_rows, value_rows]), first_mixed)
    )
    z_normed, z_spread = norm_rows(mixed_sum)
    gated_out = (z_normed * gate_float).astype(jnp.bfloat16)
    gated_part = gated_out
    out_proj = jnp.dot(
        gated_part,
        lax.all_gather(w_out, "dp", axis=0, tiled=True),
        preferred_element_type=jnp.float32,
    )
    layer_out = (out_proj + x_float).astype(jnp.bfloat16)
    d_gated = lax.dot_general(
        cotangent,
        lax.all_gather(w_out, "dp", axis=0, tiled=True),
        (((1,), (1,)), ((), ())),
        preferred_element_type=jnp.float32,
    )
    d_z_normed = d_gated * gate_float
    d_gate = d_gated * z_normed
    d_mixed = norm_back(d_z_normed, z_normed, z_spread).astype(jnp.bfloat16)
    first_query, first_key, first_value = backward_block(
        query_rows, d_mixed, own_start, key_rows, value_rows, own_start
    )

    def key_step(step_index, state_now):
        key_pair, pair_grads, query_grads = state_now
        key_pair = shifted(key_pair, "ctx", 1)
        pair_grads = shifted(pair_grads, "ctx", 1)
        source = jnp.mod(my_rank - step_index, cycle_size)
        part_query, part_key, part_value = backward_block(
            query_rows, d_mixed, own_start, key_pair[0], key_pair[1], source * tok_rows
        )
        return (key_pair, pair_grads + jnp.stack([part_key, part_value]), query_grads + part_query)

    start_state = (
        jnp.stack([key_rows, value_rows]),
        jnp.stack([first_key, first_value]),
        first_query,
    )
    unused_pair, pair_grads, d_query = lax.fori_loop(1, cycle_size, key_step, start_state)
    pair_grads = shifted(pair_grads, "ctx", 1)
    d_key = pair_grads[0]
    d_value = pair_grads[1]
    d_projected = jnp.concatenate([d_gate, d_query, d_key, d_value], axis=1)
    d_pre = (d_projected * silu_slope(pre_act)).astype(jnp.bfloat16)
    gated_part = gated_out
    in_term = lax.dot_general(
        x_normed_b, d_pre, (((0,), (0,)), ((), ())), preferred_element_type=jnp.float32
    )
    out_term = lax.dot_general(
        gated_part, cotangent, (((0,), (0,)), ((), ())), preferred_element_type=jnp.float32
    )
    owner_rows = lax.psum_scatter(
        jnp.concatenate([in_term, out_term], axis=1), "dp", scatter_dimension=0, tiled=True
    )
    owner_rows = lax.psum(owner_rows, "ctx")
    grad_in = owner_rows[:, : 4 * model_width]
    grad_out = owner_rows[:, 4 * model_width :]
    d_x_normed = lax.dot_general(
        d_pre,
        lax.all_gather(w_in, "dp", axis=0, tiled=True),
        (((1,), (1,)), ((), ())),
        preferred_element_type=jnp.float32,
    )
    d_tokens = (norm_back(d_x_normed, x_normed, x_spread) + cotangent.astype(jnp.float32)).astype(
        jnp.bfloat16
    )
    return (layer_out, d_tokens, grad_in, grad_out)


def solution(mesh):
    return jax.shard_map(
        body,
        mesh=mesh,
        in_specs=(
            P(("dp", "ctx"), None),
            P("dp", None),
            P("dp", None),
            P("dp", None),
            P(("dp", "ctx"), None),
        ),
        out_specs=(P(("dp", "ctx"), None), P(("dp", "ctx"), None), P("dp", None), P("dp", None)),
        check_vma=False,
    )
```

profile of v0, /device:TPU:4, one launch (start us, length us, event | category | flops | bytes accessed | tf_op | source)
XLA Modules:
  0.0 700.0 jit_solution(1194165250977016818)
XLA Ops:
  11.3 38.6 %all_gather.9 = bf16[512,512]{1,0:T(8,128)(2,1)S(1)} all-gather(bf16[16,512]{1,0:T(8,128)(2,1)} %param.12), channel_id=1, replica_groups=mesh['dp'=32,'ctx'=8] {'dp'}, dimensions={0}, use_global_device_ids=true | all-gather | bytes 540672 | tf_op jit(solution)/shard_map/all_gather | solution.py:149
  49.9 27.4 %all-gather.2.cloned.1.call-done = bf16[512,2048]{1,0:T(8,128)(2,1)} async-done(((bf16[16,2048]{1,0:T(8,128)(2,1)}), bf16[512,2048]{1,0:T(8,128)(2,1)}) %all-gather.2.cloned.1.call-update) | async-done | bytes 2097168 | tf_op jit(solution)/shard_map/all_gather | solution.py:122
  87.1 118.4 %while.38 = (s32[]{:T(128)}, bf16[2,256,512]{1,2,0:T(8,128)(2,1)S(1)}, f32[256,512]{0,1:T(8,128)S(1)}, s32[]{:T(128)}, s32[2]{0:T(128)S(1)}, /*index=5*/s32[]{:T...) while((s32[]{:T(128)}, ...), condition=%wide.region_7.8_spmd, body=%wide.region_4.7_spmd.sunk | while | flops 136397328 | bytes 7219506 | solution.py:141
  88.9 16.0 %collective-permute-done = bf16[2,256,512]{1,2,0:T(8,128)(2,1)S(1)} collective-permute-done((bf16[2,256,512]{1,2,0:T(8,128)(2,1)S(1)}, bf16[2,256,512]{1,2,0:T(8,128)(2,1)S(1)}, u32[]{:S(2)}, u32[]{:S(2)}) %collective-permute-start) | collective-permute-done | bytes 524320 | tf_op jit(solution)/shard_map/while/body/eval_jaxpr/ppermute | solution.py:16
  107.0 16.6 %collective-permute-done = bf16[2,256,512]{1,2,0:T(8,128)(2,1)S(1)} collective-permute-done((bf16[2,256,512]{1,2,0:T(8,128)(2,1)S(1)}, bf16[2,256,512]{1,2,0:T(8,128)(2,1)S(1)}, u32[]{:S(2)}, u32[]{:S(2)}) %collective-permute-start) | collective-permute-done | bytes 524320 | tf_op jit(solution)/shard_map/while/body/eval_jaxpr/ppermute | solution.py:16
  125.7 15.6 %collective-permute-done = bf16[2,256,512]{1,2,0:T(8,128)(2,1)S(1)} collective-permute-done((bf16[2,256,512]{1,2,0:T(8,128)(2,1)S(1)}, bf16[2,256,512]{1,2,0:T(8,128)(2,1)S(1)}, u32[]{:S(2)}, u32[]{:S(2)}) %collective-permute-start) | collective-permute-done | bytes 524320 | tf_op jit(solution)/shard_map/while/body/eval_jaxpr/ppermute | solution.py:16
  143.5 14.7 %collective-permute-done = bf16[2,256,512]{1,2,0:T(8,128)(2,1)S(1)} collective-permute-done((bf16[2,256,512]{1,2,0:T(8,128)(2,1)S(1)}, bf16[2,256,512]{1,2,0:T(8,128)(2,1)S(1)}, u32[]{:S(2)}, u32[]{:S(2)}) %collective-permute-start) | collective-permute-done | bytes 524320 | tf_op jit(solution)/shard_map/while/body/eval_jaxpr/ppermute | solution.py:16
  160.4 13.8 %collective-permute-done = bf16[2,256,512]{1,2,0:T(8,128)(2,1)S(1)} collective-permute-done((bf16[2,256,512]{1,2,0:T(8,128)(2,1)S(1)}, bf16[2,256,512]{1,2,0:T(8,128)(2,1)S(1)}, u32[]{:S(2)}, u32[]{:S(2)}) %collective-permute-start) | collective-permute-done | bytes 524320 | tf_op jit(solution)/shard_map/while/body/eval_jaxpr/ppermute | solution.py:16
  176.3 12.9 %collective-permute-done = bf16[2,256,512]{1,2,0:T(8,128)(2,1)S(1)} collective-permute-done((bf16[2,256,512]{1,2,0:T(8,128)(2,1)S(1)}, bf16[2,256,512]{1,2,0:T(8,128)(2,1)S(1)}, u32[]{:S(2)}, u32[]{:S(2)}) %collective-permute-start) | collective-permute-done | bytes 524320 | tf_op jit(solution)/shard_map/while/body/eval_jaxpr/ppermute | solution.py:16
  191.3 12.5 %collective-permute-done = bf16[2,256,512]{1,2,0:T(8,128)(2,1)S(1)} collective-permute-done((bf16[2,256,512]{1,2,0:T(8,128)(2,1)S(1)}, bf16[2,256,512]{1,2,0:T(8,128)(2,1)S(1)}, u32[]{:S(2)}, u32[]{:S(2)}) %collective-permute-start) | collective-permute-done | bytes 524320 | tf_op jit(solution)/shard_map/while/body/eval_jaxpr/ppermute | solution.py:16
  215.6 239.7 %while.39 = (s32[]{:T(128)}, bf16[2,256,512]{1,2,0:T(8,128)(2,1)}, f32[2,256,512]{1,2,0:T(8,128)}, f32[256,512]{0,1:T(8,128)S(1)}, s32[]{:T(128)}, /*index=5*/s3...) while((s32[]{:T(128)}, bf16[2,256,512]{1,2,0:T(8,128)(2,1)}, ...), condition=%wide.region_15.16_spmd, body=%wide.region_12.15_spmd.sunk | while | flops 341131776 | bytes 21440872 | solution.py:181
  215.9 18.4 %collective-permute-done.1 = bf16[2,256,512]{1,2,0:T(8,128)(2,1)S(1)} collective-permute-done((bf16[2,256,512]{1,2,0:T(8,128)(2,1)}, bf16[2,256,512]{1,2,0:T(8,128)(2,1)S(1)}, u32[]{:S(2)}, u32[]{:S(2)}) %collective-permute-start.1) | collective-permute-done | bytes 524320 | tf_op jit(solution)/shard_map/while/body/eval_jaxpr/ppermute | solution.py:16
  239.1 10.3 %collective-permute-done.2 = f32[2,256,512]{1,2,0:T(8,128)S(1)} collective-permute-done((f32[2,256,512]{1,2,0:T(8,128)}, f32[2,256,512]{1,2,0:T(8,128)S(1)}, u32[]{:S(2)}, u32[]{:S(2)}) %collective-permute-start.2) | collective-permute-done | bytes 1048608 | tf_op jit(solution)/shard_map/while/body/eval_jaxpr/ppermute | solution.py:16
  250.8 18.4 %collective-permute-done.1 = bf16[2,256,512]{1,2,0:T(8,128)(2,1)S(1)} collective-permute-done((bf16[2,256,512]{1,2,0:T(8,128)(2,1)}, bf16[2,256,512]{1,2,0:T(8,128)(2,1)S(1)}, u32[]{:S(2)}, u32[]{:S(2)}) %collective-permute-start.1) | collective-permute-done | bytes 524320 | tf_op jit(solution)/shard_map/while/body/eval_jaxpr/ppermute | solution.py:16
  285.4 18.4 %collective-permute-done.1 = bf16[2,256,512]{1,2,0:T(8,128)(2,1)S(1)} collective-permute-done((bf16[2,256,512]{1,2,0:T(8,128)(2,1)}, bf16[2,256,512]{1,2,0:T(8,128)(2,1)S(1)}, u32[]{:S(2)}, u32[]{:S(2)}) %collective-permute-start.1) | collective-permute-done | bytes 524320 | tf_op jit(solution)/shard_map/while/body/eval_jaxpr/ppermute | solution.py:16
  319.9 18.4 %collective-permute-done.1 = bf16[2,256,512]{1,2,0:T(8,128)(2,1)S(1)} collective-permute-done((bf16[2,256,512]{1,2,0:T(8,128)(2,1)}, bf16[2,256,512]{1,2,0:T(8,128)(2,1)S(1)}, u32[]{:S(2)}, u32[]{:S(2)}) %collective-permute-start.1) | collective-permute-done | bytes 524320 | tf_op jit(solution)/shard_map/while/body/eval_jaxpr/ppermute | solution.py:16
  354.5 18.4 %collective-permute-done.1 = bf16[2,256,512]{1,2,0:T(8,128)(2,1)S(1)} collective-permute-done((bf16[2,256,512]{1,2,0:T(8,128)(2,1)}, bf16[2,256,512]{1,2,0:T(8,128)(2,1)S(1)}, u32[]{:S(2)}, u32[]{:S(2)}) %collective-permute-start.1) | collective-permute-done | bytes 524320 | tf_op jit(solution)/shard_map/while/body/eval_jaxpr/ppermute | solution.py:16
  377.7 9.9 %collective-permute-done.2 = f32[2,256,512]{1,2,0:T(8,128)S(1)} collective-permute-done((f32[2,256,512]{1,2,0:T(8,128)}, f32[2,256,512]{1,2,0:T(8,128)S(1)}, u32[]{:S(2)}, u32[]{:S(2)}) %collective-permute-start.2) | collective-permute-done | bytes 1048608 | tf_op jit(solution)/shard_map/while/body/eval_jaxpr/ppermute | solution.py:16
  389.0 17.9 %collective-permute-done.1 = bf16[2,256,512]{1,2,0:T(8,128)(2,1)S(1)} collective-permute-done((bf16[2,256,512]{1,2,0:T(8,128)(2,1)}, bf16[2,256,512]{1,2,0:T(8,128)(2,1)S(1)}, u32[]{:S(2)}, u32[]{:S(2)}) %collective-permute-start.1) | collective-permute-done | bytes 524320 | tf_op jit(solution)/shard_map/while/body/eval_jaxpr/ppermute | solution.py:16
  411.8 10.4 %collective-permute-done.2 = f32[2,256,512]{1,2,0:T(8,128)S(1)} collective-permute-done((f32[2,256,512]{1,2,0:T(8,128)}, f32[2,256,512]{1,2,0:T(8,128)S(1)}, u32[]{:S(2)}, u32[]{:S(2)}) %collective-permute-start.2) | collective-permute-done | bytes 1048608 | tf_op jit(solution)/shard_map/while/body/eval_jaxpr/ppermute | solution.py:16
  423.6 17.1 %collective-permute-done.1 = bf16[2,256,512]{1,2,0:T(8,128)(2,1)S(1)} collective-permute-done((bf16[2,256,512]{1,2,0:T(8,128)(2,1)}, bf16[2,256,512]{1,2,0:T(8,128)(2,1)S(1)}, u32[]{:S(2)}, u32[]{:S(2)}) %collective-permute-start.1) | collective-permute-done | bytes 524320 | tf_op jit(solution)/shard_map/while/body/eval_jaxpr/ppermute | solution.py:16
  458.4 18.2 %collective-permute-done.3 = f32[2,256,512]{2,1,0:T(8,128)} collective-permute-done((f32[2,256,512]{2,1,0:T(8,128)}, f32[2,256,512]{2,1,0:T(8,128)}, u32[]{:S(2)}, u32[]{:S(2)}) %collective-permute-start.3) | collective-permute-done | bytes 1048608 | tf_op jit(solution)/shard_map/ppermute | solution.py:16
  486.1 119.2 %reduce-scatter.2.cloned.1.call-done = f32[16,2560]{1,0:T(8,128)} async-done(((f32[512,2560]{1,0:T(8,128)}), f32[16,2560]{1,0:T(8,128)}) %reduce-scatter.2.cloned.1.call-update) | async-done | bytes 163856 | tf_op jit(solution)/shard_map/reduce_scatter | solution.py:194
  606.2 84.3 %all-reduce.2.cloned.1.call-done = f32[16,2560]{1,0:T(8,128)} async-done(((f32[16,2560]{1,0:T(8,128)}), f32[16,2560]{1,0:T(8,128)}) %all-reduce.2.cloned.1.call-update) | async-done | bytes 163856 | tf_op jit(solution)/shard_map/psum | solution.py:197
  (237 shorter events, 137.7 us)
Async XLA Ops:
  7.2 70.1 %all-gather.2.cloned.1.call-start = ((), (), s32[]{:S(2)}) async-start(), calls=%async_computation.1 | async-start | bytes 2162688 | tf_op jit(solution)/shard_map/all_gather | solution.py:122
  7.9 597.3 %reduce-scatter.2.cloned.1.call-start = ((), (), s32[]{:S(2)}) async-start(), calls=%async_computation.2 | async-start | bytes 5406720 | tf_op jit(solution)/shard_map/reduce_scatter | solution.py:194
  87.1 17.8 %collective-permute-start = (bf16[2,256,512]{1,2,0:T(8,128)(2,1)S(1)}, bf16[2,256,512]{1,2,0:T(8,128)(2,1)S(1)}, u32[]{:S(2)}, u32[]{:S(2)}) collective-permute-start(bf16[2,256,512]{1,2,0:T(8,128)(2,1)S(1)} %get-tuple-element.733), channel_id=1, source_target_pairs={{0,1},{1,2},{2,3},{3,4},{4,5},{5,6},{6,7},{7,0},{8,9},{9,10},{10,1... | collective-permute-start | bytes 1572872 | tf_op jit(solution)/shard_map/while/body/eval_jaxpr/ppermute | solution.py:16
  106.7 16.9 %collective-permute-start = (bf16[2,256,512]{1,2,0:T(8,128)(2,1)S(1)}, bf16[2,256,512]{1,2,0:T(8,128)(2,1)S(1)}, u32[]{:S(2)}, u32[]{:S(2)}) collective-permute-start(bf16[2,256,512]{1,2,0:T(8,128)(2,1)S(1)} %get-tuple-element.733), channel_id=1, source_target_pairs={{0,1},{1,2},{2,3},{3,4},{4,5},{5,6},{6,7},{7,0},{8,9},{9,10},{10,1... | collective-permute-start | bytes 1572872 | tf_op jit(solution)/shard_map/while/body/eval_jaxpr/ppermute | solution.py:16
  125.4 16.0 %collective-permute-start = (bf16[2,256,512]{1,2,0:T(8,128)(2,1)S(1)}, bf16[2,256,512]{1,2,0:T(8,128)(2,1)S(1)}, u32[]{:S(2)}, u32[]{:S(2)}) collective-permute-start(bf16[2,256,512]{1,2,0:T(8,128)(2,1)S(1)} %get-tuple-element.733), channel_id=1, source_target_pairs={{0,1},{1,2},{2,3},{3,4},{4,5},{5,6},{6,7},{7,0},{8,9},{9,10},{10,1... | collective-permute-start | bytes 1572872 | tf_op jit(solution)/shard_map/while/body/eval_jaxpr/ppermute | solution.py:16
  143.1 15.1 %collective-permute-start = (bf16[2,256,512]{1,2,0:T(8,128)(2,1)S(1)}, bf16[2,256,512]{1,2,0:T(8,128)(2,1)S(1)}, u32[]{:S(2)}, u32[]{:S(2)}) collective-permute-start(bf16[2,256,512]{1,2,0:T(8,128)(2,1)S(1)} %get-tuple-element.733), channel_id=1, source_target_pairs={{0,1},{1,2},{2,3},{3,4},{4,5},{5,6},{6,7},{7,0},{8,9},{9,10},{10,1... | collective-permute-start | bytes 1572872 | tf_op jit(solution)/shard_map/while/body/eval_jaxpr/ppermute | solution.py:16
  160.0 14.2 %collective-permute-start = (bf16[2,256,512]{1,2,0:T(8,128)(2,1)S(1)}, bf16[2,256,512]{1,2,0:T(8,128)(2,1)S(1)}, u32[]{:S(2)}, u32[]{:S(2)}) collective-permute-start(bf16[2,256,512]{1,2,0:T(8,128)(2,1)S(1)} %get-tuple-element.733), channel_id=1, source_target_pairs={{0,1},{1,2},{2,3},{3,4},{4,5},{5,6},{6,7},{7,0},{8,9},{9,10},{10,1... | collective-permute-start | bytes 1572872 | tf_op jit(solution)/shard_map/while/body/eval_jaxpr/ppermute | solution.py:16
  175.9 13.2 %collective-permute-start = (bf16[2,256,512]{1,2,0:T(8,128)(2,1)S(1)}, bf16[2,256,512]{1,2,0:T(8,128)(2,1)S(1)}, u32[]{:S(2)}, u32[]{:S(2)}) collective-permute-start(bf16[2,256,512]{1,2,0:T(8,128)(2,1)S(1)} %get-tuple-element.733), channel_id=1, source_target_pairs={{0,1},{1,2},{2,3},{3,4},{4,5},{5,6},{6,7},{7,0},{8,9},{9,10},{10,1... | collective-permute-start | bytes 1572872 | tf_op jit(solution)/shard_map/while/body/eval_jaxpr/ppermute | solution.py:16
  215.6 18.7 %collective-permute-start.1 = (bf16[2,256,512]{1,2,0:T(8,128)(2,1)}, bf16[2,256,512]{1,2,0:T(8,128)(2,1)S(1)}, u32[]{:S(2)}, u32[]{:S(2)}) collective-permute-start(bf16[2,256,512]{1,2,0:T(8,128)(2,1)} %get-tuple-element.771), channel_id=1, source_target_pairs={{0,1},{1,2},{2,3},{3,4},{4,5},{5,6},{6,7},{7,0},{8,9},{9,10},{10,1... | collective-permute-start | bytes 1572872 | tf_op jit(solution)/shard_map/while/body/eval_jaxpr/ppermute | solution.py:16
  215.6 33.8 %collective-permute-start.2 = (f32[2,256,512]{1,2,0:T(8,128)}, f32[2,256,512]{1,2,0:T(8,128)S(1)}, u32[]{:S(2)}, u32[]{:S(2)}) collective-permute-start(f32[2,256,512]{1,2,0:T(8,128)} %get-tuple-element.772), channel_id=1, source_target_pairs={{0,1},{1,2},{2,3},{3,4},{4,5},{5,6},{6,7},{7,0},{8,9},{9,10},{10,1... | collective-permute-start | bytes 3145736 | tf_op jit(solution)/shard_map/while/body/eval_jaxpr/ppermute | solution.py:16
  250.5 18.7 %collective-permute-start.1 = (bf16[2,256,512]{1,2,0:T(8,128)(2,1)}, bf16[2,256,512]{1,2,0:T(8,128)(2,1)S(1)}, u32[]{:S(2)}, u32[]{:S(2)}) collective-permute-start(bf16[2,256,512]{1,2,0:T(8,128)(2,1)} %get-tuple-element.771), channel_id=1, source_target_pairs={{0,1},{1,2},{2,3},{3,4},{4,5},{5,6},{6,7},{7,0},{8,9},{9,10},{10,1... | collective-permute-start | bytes 1572872 | tf_op jit(solution)/shard_map/while/body/eval_jaxpr/ppermute | solution.py:16
  250.5 33.4 %collective-permute-start.2 = (f32[2,256,512]{1,2,0:T(8,128)}, f32[2,256,512]{1,2,0:T(8,128)S(1)}, u32[]{:S(2)}, u32[]{:S(2)}) collective-permute-start(f32[2,256,512]{1,2,0:T(8,128)} %get-tuple-element.772), channel_id=1, source_target_pairs={{0,1},{1,2},{2,3},{3,4},{4,5},{5,6},{6,7},{7,0},{8,9},{9,10},{10,1... | collective-permute-start | bytes 3145736 | tf_op jit(solution)/shard_map/while/body/eval_jaxpr/ppermute | solution.py:16
  285.1 18.7 %collective-permute-start.1 = (bf16[2,256,512]{1,2,0:T(8,128)(2,1)}, bf16[2,256,512]{1,2,0:T(8,128)(2,1)S(1)}, u32[]{:S(2)}, u32[]{:S(2)}) collective-permute-start(bf16[2,256,512]{1,2,0:T(8,128)(2,1)} %get-tuple-element.771), channel_id=1, source_target_pairs={{0,1},{1,2},{2,3},{3,4},{4,5},{5,6},{6,7},{7,0},{8,9},{9,10},{10,1... | collective-permute-start | bytes 1572872 | tf_op jit(solution)/shard_map/while/body/eval_jaxpr/ppermute | solution.py:16
  285.1 33.4 %collective-permute-start.2 = (f32[2,256,512]{1,2,0:T(8,128)}, f32[2,256,512]{1,2,0:T(8,128)S(1)}, u32[]{:S(2)}, u32[]{:S(2)}) collective-permute-start(f32[2,256,512]{1,2,0:T(8,128)} %get-tuple-element.772), channel_id=1, source_target_pairs={{0,1},{1,2},{2,3},{3,4},{4,5},{5,6},{6,7},{7,0},{8,9},{9,10},{10,1... | collective-permute-start | bytes 3145736 | tf_op jit(solution)/shard_map/while/body/eval_jaxpr/ppermute | solution.py:16
  319.6 18.7 %collective-permute-start.1 = (bf16[2,256,512]{1,2,0:T(8,128)(2,1)}, bf16[2,256,512]{1,2,0:T(8,128)(2,1)S(1)}, u32[]{:S(2)}, u32[]{:S(2)}) collective-permute-start(bf16[2,256,512]{1,2,0:T(8,128)(2,1)} %get-tuple-element.771), channel_id=1, source_target_pairs={{0,1},{1,2},{2,3},{3,4},{4,5},{5,6},{6,7},{7,0},{8,9},{9,10},{10,1... | collective-permute-start | bytes 1572872 | tf_op jit(solution)/shard_map/while/body/eval_jaxpr/ppermute | solution.py:16
  319.6 33.4 %collective-permute-start.2 = (f32[2,256,512]{1,2,0:T(8,128)}, f32[2,256,512]{1,2,0:T(8,128)S(1)}, u32[]{:S(2)}, u32[]{:S(2)}) collective-permute-start(f32[2,256,512]{1,2,0:T(8,128)} %get-tuple-element.772), channel_id=1, source_target_pairs={{0,1},{1,2},{2,3},{3,4},{4,5},{5,6},{6,7},{7,0},{8,9},{9,10},{10,1... | collective-permute-start | bytes 3145736 | tf_op jit(solution)/shard_map/while/body/eval_jaxpr/ppermute | solution.py:16
  354.2 18.7 %collective-permute-start.1 = (bf16[2,256,512]{1,2,0:T(8,128)(2,1)}, bf16[2,256,512]{1,2,0:T(8,128)(2,1)S(1)}, u32[]{:S(2)}, u32[]{:S(2)}) collective-permute-start(bf16[2,256,512]{1,2,0:T(8,128)(2,1)} %get-tuple-element.771), channel_id=1, source_target_pairs={{0,1},{1,2},{2,3},{3,4},{4,5},{5,6},{6,7},{7,0},{8,9},{9,10},{10,1... | collective-permute-start | bytes 1572872 | tf_op jit(solution)/shard_map/while/body/eval_jaxpr/ppermute | solution.py:16
  354.2 33.4 %collective-permute-start.2 = (f32[2,256,512]{1,2,0:T(8,128)}, f32[2,256,512]{1,2,0:T(8,128)S(1)}, u32[]{:S(2)}, u32[]{:S(2)}) collective-permute-start(f32[2,256,512]{1,2,0:T(8,128)} %get-tuple-element.772), channel_id=1, source_target_pairs={{0,1},{1,2},{2,3},{3,4},{4,5},{5,6},{6,7},{7,0},{8,9},{9,10},{10,1... | collective-permute-start | bytes 3145736 | tf_op jit(solution)/shard_map/while/body/eval_jaxpr/ppermute | solution.py:16
  388.8 18.2 %collective-permute-start.1 = (bf16[2,256,512]{1,2,0:T(8,128)(2,1)}, bf16[2,256,512]{1,2,0:T(8,128)(2,1)S(1)}, u32[]{:S(2)}, u32[]{:S(2)}) collective-permute-start(bf16[2,256,512]{1,2,0:T(8,128)(2,1)} %get-tuple-element.771), channel_id=1, source_target_pairs={{0,1},{1,2},{2,3},{3,4},{4,5},{5,6},{6,7},{7,0},{8,9},{9,10},{10,1... | collective-permute-start | bytes 1572872 | tf_op jit(solution)/shard_map/while/body/eval_jaxpr/ppermute | solution.py:16
  388.8 33.4 %collective-permute-start.2 = (f32[2,256,512]{1,2,0:T(8,128)}, f32[2,256,512]{1,2,0:T(8,128)S(1)}, u32[]{:S(2)}, u32[]{:S(2)}) collective-permute-start(f32[2,256,512]{1,2,0:T(8,128)} %get-tuple-element.772), channel_id=1, source_target_pairs={{0,1},{1,2},{2,3},{3,4},{4,5},{5,6},{6,7},{7,0},{8,9},{9,10},{10,1... | collective-permute-start | bytes 3145736 | tf_op jit(solution)/shard_map/while/body/eval_jaxpr/ppermute | solution.py:16
  423.3 17.4 %collective-permute-start.1 = (bf16[2,256,512]{1,2,0:T(8,128)(2,1)}, bf16[2,256,512]{1,2,0:T(8,128)(2,1)S(1)}, u32[]{:S(2)}, u32[]{:S(2)}) collective-permute-start(bf16[2,256,512]{1,2,0:T(8,128)(2,1)} %get-tuple-element.771), channel_id=1, source_target_pairs={{0,1},{1,2},{2,3},{3,4},{4,5},{5,6},{6,7},{7,0},{8,9},{9,10},{10,1... | collective-permute-start | bytes 1572872 | tf_op jit(solution)/shard_map/while/body/eval_jaxpr/ppermute | solution.py:16
  423.3 30.9 %collective-permute-start.2 = (f32[2,256,512]{1,2,0:T(8,128)}, f32[2,256,512]{1,2,0:T(8,128)S(1)}, u32[]{:S(2)}, u32[]{:S(2)}) collective-permute-start(f32[2,256,512]{1,2,0:T(8,128)} %get-tuple-element.772), channel_id=1, source_target_pairs={{0,1},{1,2},{2,3},{3,4},{4,5},{5,6},{6,7},{7,0},{8,9},{9,10},{10,1... | collective-permute-start | bytes 3145736 | tf_op jit(solution)/shard_map/while/body/eval_jaxpr/ppermute | solution.py:16
  457.9 18.7 %collective-permute-start.3 = (f32[2,256,512]{2,1,0:T(8,128)}, f32[2,256,512]{2,1,0:T(8,128)}, u32[]{:S(2)}, u32[]{:S(2)}) collective-permute-start(f32[2,256,512]{2,1,0:T(8,128)} %copy.69), channel_id=1, source_target_pairs={{0,1},{1,2},{2,3},{3,4},{4,5},{5,6},{6,7},{7,0},{8,9},{9,10},{10,1... | collective-permute-start | bytes 3145736 | tf_op jit(solution)/shard_map/ppermute | solution.py:16
  482.5 208.0 %all-reduce.2.cloned.1.call-start = ((), (), s32[]{:S(2)}) async-start(), calls=%async_computation.3 | async-start | bytes 327680 | tf_op jit(solution)/shard_map/psum | solution.py:197
  (11 other events, 74.2 us)
Sparse Core Ops, SparseCore 0:
  9.9 67.3 all-gather.1
  482.6 122.5 reduce-scatter.1
  607.9 82.5 all-reduce.1
where the time goes:
time: 703 us; the launch traced here: 700 us
  waiting for transfers between devices  548 us (78%)
  matrix products  53.1 us (8%)
  blocking collectives  38.6 us (5%)
  other arithmetic  24 us (3%)
  local copies, waits for them, and re-layouts  19.1 us (3%)
  between operations  14 us (2%)
    ppermute x22, waiting for transfers between devices, shifted(): lax.ppermute(shard, axis, [(i, (i + by) % count) for i in range(count)])  316 us
    reduce_scatter x1, waiting for transfers between devices, body(): lax.psum_scatter(jnp.concatenate([in_term, out_term], axis=1), 'dp', scat...  119 us
    psum x1, waiting for transfers between devices, body(): owner_rows = lax.psum(owner_rows, 'ctx')  84.3 us
    all_gather x1, blocking collectives, body(): lax.all_gather(w_out, 'dp', axis=0, tiled=True)  38.6 us
    all_gather x1, waiting for transfers between devices, body(): w_whole = lax.all_gather(w_in, 'dp', axis=0, tiled=True)  27.4 us
  transfers between devices with their start and end apart: 25, of which 25 were waited for; matrix products, arithmetic and copies ran while one was open for 6% of the time, Pallas kernels for 0%

commit v1 on v0

v1 whole, which is shorter than its diff:
```python
import math

import jax
import jax.numpy as jnp
from jax import lax
from jax.experimental import pallas as pl
from jax.experimental.pallas import tpu as pltpu
from jax.sharding import PartitionSpec as P

MESH = pl.DeviceIdType.MESH
F32 = jnp.float32
BF16 = jnp.bfloat16
EPS = 1e-05
NZ = 8
D = 512
H = 128
SCALE = 1.0 / math.sqrt(H)
NN = (((1,), (0,)), ((), ()))
NT = (((1,), (1,)), ((), ()))
BASE = (0, 4, 7, 9)


def dot(lhs, rhs, dims=NN):
    return lax.dot_general(lhs, rhs, dims, preferred_element_type=F32)


def sigmoid(v):
    return 0.5 * jnp.tanh(0.5 * v) + 0.5


def kernel(
    tok, seq, win, wout, cot, lo_out, dt_out, gi_out, go_out,
    xa, ca, xt, w5, wo5, wgt, kv, kvt, qs, slope, gate_t, slope_gt, dg_t, dz_t,
    at, sl, mixed_t, stats, dm_t, z_t, dq_t, dkv_own, dkv_far, dkv_s, dkv_r,
    lo_f, lo_s, lo_r, dpre, dx_f, dx_s, dx_r,
    ga, gb, s1, r1, s2, r2, tot, s3, r3, fr,
    go, os1, or1, os2, or2, otot, os3, or3, ofr,
    ssem, rsem,
):
    dp = lax.axis_index("dp")
    cx = lax.axis_index("ctx")
    z, xl, k = dp // 4, (dp // 2) % 2, dp % 2
    a, y = cx // 4, cx % 4
    x = a * 2 + xl

    def at_y(s):
        return {"dp": dp, "ctx": a * 4 + (y + s) % 4}

    def at_x(s):
        there = (x + s) % 4
        return {"dp": z * 4 + (there % 2) * 2 + k, "ctx": (there // 2) * 4 + y}

    def at_z(s):
        return {"dp": ((z + s) % NZ) * 4 + xl * 2 + k, "ctx": cx}

    def at_zabs(there):
        return {"dp": there * 4 + xl * 2 + k, "ctx": cx}

    def at_ctx(s):
        return {"dp": dp, "ctx": (cx + s) % 8}

    core = {"dp": z * 4 + xl * 2 + (1 - k), "ctx": cx}
    xl_mate = {"dp": z * 4 + (1 - xl) * 2 + k, "ctx": cx}
    far = {"dp": dp, "ctx": (1 - a) * 4 + y}

    peers = [core, at_x(1), at_x(3)]
    peers += [at_z(s) for s in range(1, NZ)]
    peers += [at_ctx(s) for s in range(1, 8)]
    barrier = pltpu.get_barrier_semaphore()
    for peer in peers:
        pl.semaphore_signal(barrier, inc=1, device_id=peer, device_id_type=MESH)

    counter = [0]
    started = []

    def sems(n=1):
        first = counter[0]
        counter[0] += n
        return first

    def remote(src, dst, peer, s_index, r_index):
        return pltpu.make_async_remote_copy(
            src_ref=src, dst_ref=dst, send_sem=ssem.at[s_index], recv_sem=rsem.at[r_index],
            device_id=peer, device_id_type=MESH,
        )

    def send(src, dst, peer):
        i = sems()
        copy = remote(src, dst, peer, i, i)
        copy.start()
        started.append(copy)
        return copy

    def arrive(copies):
        for copy in copies:
            copy.wait_recv()

    early = pl.ds(pl.multiple_of(y * 128, 128), 128)
    late = pl.ds(pl.multiple_of((7 - y) * 128, 128), 128)

    def slots(s):
        there = (y + s) % 4
        return (
            pl.ds(pl.multiple_of(there * 128, 128), 128),
            pl.ds(pl.multiple_of((7 - there) * 128, 128), 128),
        )

    for part in range(4):
        w5[z, xl, k, :, part * 128 : (part + 1) * 128] = win[
            :, pl.ds(pl.multiple_of(part * D + y * 128, 128), 128)
        ]
    owner = z // 2 == y

    @pl.when(owner)
    def _():
        wo5[z % 2, xl, k] = wout[...]

    def normed(rows):
        v = tok[rows, :].astype(F32)
        centre = v - jnp.mean(v, axis=-1, keepdims=True)
        spread = lax.rsqrt(jnp.mean(centre * centre, axis=-1, keepdims=True) + EPS)
        return centre * spread, spread

    xa[early, :] = normed(pl.ds(0, 128))[0].astype(BF16)
    xa[late, :] = normed(pl.ds(128, 128))[0].astype(BF16)
    ca[early, :] = cot[0:128, :]
    ca[late, :] = cot[128:256, :]

    pl.semaphore_wait(barrier, len(peers))

    w_z = [send(w5.at[z, xl, k], w5.at[z, xl, k], at_z(s)) for s in range(1, NZ)]
    x_y = []
    for s in (1, 3, 2):
        x_y.append(send(xa.at[early], xa.at[early], at_y(s)))
        x_y.append(send(xa.at[late], xa.at[late], at_y(s)))
    wo_first = sems(NZ)

    def wo_copy(s):
        return remote(
            wo5.at[z % 2, xl, k], wo5.at[z % 2, xl, k], at_z(s), wo_first + s, wo_first + z % 2
        )

    @pl.when(owner)
    def _():
        for s in range(1, NZ):
            wo_copy(s).start()

    arrive(w_z)
    w_x = send(w5.at[:, xl, k], w5.at[:, xl, k], xl_mate)

    for j in range(2):
        @pl.when(z != 2 * y + j)
        def _():
            remote(
                wo5.at[j, xl, k], wo5.at[j, xl, k], at_z(1), wo_first, wo_first + j
            ).wait_recv()

    wo_x = send(wo5.at[:, xl, k], wo5.at[:, xl, k], xl_mate)
    arrive([w_x])
    w_k = send(w5.at[:, :, k], w5.at[:, :, k], core)
    arrive([wo_x])
    wo_k = send(wo5.at[:, :, k], wo5.at[:, :, k], core)
    arrive([w_k])
    arrive(x_y)
    c_y = []
    for s in (1, 3, 2):
        c_y.append(send(ca.at[early], ca.at[early], at_y(s)))
        c_y.append(send(ca.at[late], ca.at[late], at_y(s)))

    kv_x = []
    for i in range(4):
        rows = pl.ds(i * 256, 256)
        pre = dot(xa[rows, :], w5[:, :, :, :, 256:512].reshape(D, 256))
        sig = sigmoid(pre)
        act = pre * sig
        kv[a, rows, :] = act.astype(BF16)
        slope[rows, 128:384] = sig + act * (1.0 - sig)
        kv_x.append(send(kv.at[a, rows], kv.at[a, rows], far))
    wgt[...] = w5[:, :, :, :, 0:128].reshape(D, 128).T
    for i in range(4):
        rows = pl.ds(i * 256, 256)
        pre = dot(xa[rows, :], w5[:, :, :, :, 128:256].reshape(D, 128))
        sig = sigmoid(pre)
        act = pre * sig
        qs[rows, :] = act.astype(BF16)
        slope[rows, 0:128] = sig + act * (1.0 - sig)
        pre = dot(wgt[...], xa[rows, :], NT)
        sig = sigmoid(pre)
        act = pre * sig
        gate_t[:, rows] = act.astype(BF16).astype(F32)
        slope_gt[:, rows] = sig + act * (1.0 - sig)
        kvt[a, :, rows] = kv[a, rows, :].T
        xt[:, rows] = xa[rows, :].T

    mixed_t[...] = jnp.zeros_like(mixed_t)
    border = seq[0, 0]

    def tile(i):
        return pl.ds(pl.multiple_of(i * 256, 256), 256)

    def place(half, i):
        return i * 256 + half * 512 + (1 - half) * 1024 * (i // 2)

    def attend(half, kt, qt, index, diagonal):
        scores = dot(kv[half, tile(kt), 0:128], qs[tile(qt), :], NT)
        key_at = lax.broadcasted_iota(jnp.int32, (256, 256), 0) + place(half, kt)
        query_at = lax.broadcasted_iota(jnp.int32, (1, 256), 1) + place(a, qt)
        least = jnp.where(query_at >= border, border, 0)
        allowed = key_at >= least
        if diagonal:
            allowed = allowed & (key_at <= query_at)
        s = scores * SCALE
        sig = jnp.where(allowed, sigmoid(s), 0.0)
        act = s * sig
        act_b = act.astype(BF16)
        at[index] = act_b
        sl[index] = sig + act * (1.0 - sig)
        mixed_t[:, tile(qt)] += dot(kvt[half, 128:256, tile(kt)], act_b)

    for kt in range(4):
        attend(a, kt, kt, BASE[kt], True)
        if kt < 3:
            def step(qt, carry, kt=kt):
                attend(a, kt, qt, BASE[kt] + qt - kt, False)
                return carry

            lax.fori_loop(kt + 1, 4, step, 0)

    arrive(c_y)
    arrive([wo_k])
    for i in range(4):
        rows = pl.ds(i * 256, 256)
        part = dot(wo5[...].reshape(128, D), ca[rows, :], NT)
        dg_t[:, rows] = part
        dz_t[:, rows] = part * gate_t[:, rows]

    arrive(kv_x)
    for i in range(4):
        rows = pl.ds(i * 256, 256)
        kvt[1 - a, :, rows] = kv[1 - a, rows, :].T

    def far_tiles(t):
        return t // (2 + 2 * a), t % (2 + 2 * a) + 2 * (1 - a)

    def far_step(t, carry):
        kt, qt = far_tiles(t)
        attend(1 - a, kt, qt, 10 + t, False)
        return carry

    lax.fori_loop(0, 8, far_step, 0)

    mixed = mixed_t[...]
    mean_h = jnp.mean(mixed, axis=0, keepdims=True)
    centred = mixed - mean_h
    dz = dz_t[...]
    stats[y, 0:1, :] = mean_h
    stats[y, 1:2, :] = jnp.sum(centred * centred, axis=0, keepdims=True)
    stats[y, 2:3, :] = jnp.sum(dz, axis=0, keepdims=True)
    stats[y, 3:4, :] = jnp.sum(dz * centred, axis=0, keepdims=True)
    stats[y, 4:8, :] = jnp.zeros((4, 1024), F32)
    arrive([send(stats.at[y], stats.at[y], at_y(s)) for s in (1, 2, 3)])
    means = [stats[j, 0:1, :] for j in range(4)]
    mean = (means[0] + means[1] + means[2] + means[3]) * 0.25
    second = jnp.zeros((1, 1024), F32)
    first_dz = jnp.zeros((1, 1024), F32)
    second_dz = jnp.zeros((1, 1024), F32)
    for j in range(4):
        off = means[j] - mean
        second += stats[j, 1:2, :] + 128.0 * off * off
        first_dz += stats[j, 2:3, :]
        second_dz += stats[j, 3:4, :] + off * stats[j, 2:3, :]
    spread = lax.rsqrt(second * (1.0 / D) + EPS)
    first_dz = first_dz * (1.0 / D)
    second_dz = second_dz * (1.0 / D) * spread
    for i in range(4):
        rows = pl.ds(i * 256, 256)
        r = spread[:, i * 256 : (i + 1) * 256]
        zn = (mixed_t[:, rows] - mean[:, i * 256 : (i + 1) * 256]) * r
        z_t[:, rows] = (zn * gate_t[:, rows]).astype(BF16)
        dm_t[:, rows] = (
            r * (
                dz_t[:, rows] - first_dz[:, i * 256 : (i + 1) * 256]
                - zn * second_dz[:, i * 256 : (i + 1) * 256]
            )
        ).astype(BF16)
        dpre[rows, 0:128] = (dg_t[:, rows] * zn * slope_gt[:, rows]).astype(BF16).T

    dq_t[...] = jnp.zeros_like(dq_t)
    dkv_own[...] = jnp.zeros_like(dkv_own)
    dkv_far[...] = jnp.zeros_like(dkv_far)

    def attend_back(half, kt, qt, index, grads):
        d_attn = dot(kv[half, tile(kt), 128:256], dm_t[:, tile(qt)])
        ds = (d_attn * sl[index]).astype(BF16)
        grads[tile(kt), 128:256] += dot(at[index], dm_t[:, tile(qt)], NT)
        grads[tile(kt), 0:128] += dot(ds, qs[tile(qt), :])
        dq_t[:, tile(qt)] += dot(kvt[half, 0:128, tile(kt)], ds)

    def far_back(t, carry):
        kt, qt = far_tiles(t)
        attend_back(1 - a, kt, qt, 10 + t, dkv_far)
        return carry

    lax.fori_loop(0, 8, far_back, 0)
    dkv_x = []
    for i in range(4):
        rows = pl.ds(i * 256, 256)
        dkv_s[rows, :] = dkv_far[rows, :].astype(BF16)
        dkv_x.append(send(dkv_s.at[rows], dkv_r.at[rows], far))

    for i in range(4):
        rows = pl.ds(i * 256, 256)
        part = dot(z_t[:, rows].T, wo5[...].reshape(128, D))
        lo_f[rows, :] = part
        lo_s[rows, :] = part.astype(BF16)
    lo_y = []
    for s in (1, 3, 2):
        to_early, to_late = slots(s)
        lo_y.append(send(lo_s.at[to_early], lo_r.at[s - 1, pl.ds(0, 128)], at_y(s)))
        lo_y.append(send(lo_s.at[to_late], lo_r.at[s - 1, pl.ds(128, 128)], at_y(s)))
    go[...] = dot(z_t[...], ca[...]).reshape(2, 2, 2, 16, D)
    os1[...] = go[:, :, 1 - k].astype(BF16)
    go_k = send(os1, or1, core)

    for kt in range(4):
        def back_step(qt, carry, kt=kt):
            attend_back(a, kt, qt, BASE[kt] + qt - kt, dkv_own)
            return carry

        lax.fori_loop(kt, 4, back_step, 0)

    arrive([go_k])
    go[:, :, k] = go[:, :, k] + or1[...].astype(F32)
    for there in range(4):
        os2[there] = go[:, there % 2, k, :, (there // 2) * 256 : (there // 2 + 1) * 256].astype(BF16)
    go_x = [send(os2.at[(x + s) % 4], or2.at[s - 1], at_x(s)) for s in (1, 2, 3)]

    for i in range(4):
        rows = pl.ds(i * 256, 256)
        dpre[rows, 128:256] = ((dq_t[:, rows] * SCALE).T * slope[rows, 0:128]).astype(BF16)

    def grad_start(grads, first_column, n):
        for i in range(2):
            rows = pl.ds(i * 256, 256)
            part = dot(xt[rows, :], dpre[:, first_column : first_column + 256])
            grads[i * 4 : (i + 1) * 4] = part.reshape(4, 2, 2, 16, 256)
        s1[n] = grads[:, :, 1 - k].astype(BF16)
        return send(s1.at[n], r1.at[n], core)

    def grad_x(grads, n, copy):
        arrive([copy])
        grads[:, :, k] = grads[:, :, k] + r1[n].astype(F32)
        for there in range(4):
            s2[n, there] = grads[
                :, there % 2, k, :, (there // 2) * 128 : (there // 2 + 1) * 128
            ].astype(BF16)
        return [send(s2.at[n, (x + s) % 4], r2.at[n, s - 1], at_x(s)) for s in (1, 2, 3)]

    def grad_z(grads, n, copies):
        arrive(copies)
        total = grads[:, xl, k, :, pl.ds(pl.multiple_of(a * 128, 128), 128)]
        total = total + r2[n, 0].astype(F32) + r2[n, 1].astype(F32) + r2[n, 2].astype(F32)
        tot[n] = total
        s3[n] = total.astype(BF16)
        return [send(s3.at[n, (z + s) % NZ], r3.at[n, s - 1], at_z(s)) for s in range(1, NZ)]

    def grad_ctx(n, copies):
        arrive(copies)
        total = tot[n, z]
        for s in range(NZ - 1):
            total = total + r3[n, s].astype(F32)
        fr[n, cx] = total
        return [send(fr.at[n, cx], fr.at[n, cx], at_ctx(s)) for s in range(1, 8)]

    def grad_end(n, copies):
        arrive(copies)
        for c in range(8):
            first = (n * 2 + c // 4) * D + (c % 4) * 128
            gi_out[:, first : first + 128] = fr[n, c]

    ga_k = grad_start(ga, 0, 0)

    arrive(go_x)
    total = go[:, xl, k, :, pl.ds(pl.multiple_of(a * 256, 256), 256)]
    total = total + or2[0].astype(F32) + or2[1].astype(F32) + or2[2].astype(F32)
    otot[...] = total
    os3[...] = total.astype(BF16)
    go_first = sems(NZ)
    go_sent = sems(2)

    def go_copy(j):
        return remote(os3.at[j], or3.at[z], at_zabs(2 * y + j), go_sent + j, go_first + z)

    for j in range(2):
        @pl.when(z != 2 * y + j)
        def _():
            go_copy(j).start()

    ga_x = grad_x(ga, 0, ga_k)
    go_end_first = sems(8)
    go_end_recv = sems(2)

    def go_end(s):
        return remote(ofr.at[a], ofr.at[a], at_ctx(s), go_end_first + s, go_end_recv + a)

    @pl.when(owner)
    def _():
        final = otot[z % 2]
        for s in range(1, NZ):
            source = (z + s) % NZ
            remote(
                os3.at[0], or3.at[source], at_z(s), go_sent, go_first + source
            ).wait_recv()
            final = final + or3[source].astype(F32)
        ofr[a] = final
        for s in range(1, 8):
            go_end(s).start()

    ga_z = grad_z(ga, 0, ga_x)

    for i in range(4):
        rows = pl.ds(i * 256, 256)
        arrive([dkv_x[i]])
        both = dkv_own[rows, :] + dkv_r[rows, :].astype(F32)
        dpre[rows, 256:384] = (both[:, 0:128] * SCALE * slope[rows, 128:256]).astype(BF16)
        dpre[rows, 384:512] = (both[:, 128:256] * slope[rows, 256:384]).astype(BF16)
        part = dot(dpre[rows, :], w5[...].reshape(D, D), NT)
        dx_f[rows, :] = part
        dx_s[rows, :] = part.astype(BF16)
    dx_y = []
    for s in (1, 3, 2):
        to_early, to_late = slots(s)
        dx_y.append(send(dx_s.at[to_early], dx_r.at[s - 1, pl.ds(0, 128)], at_y(s)))
        dx_y.append(send(dx_s.at[to_late], dx_r.at[s - 1, pl.ds(128, 128)], at_y(s)))
    gb_k = grad_start(gb, 256, 1)
    ga_c = grad_ctx(0, ga_z)
    gb_x = grad_x(gb, 1, gb_k)

    arrive(lo_y)
    for i, rows in enumerate((early, late)):
        own = pl.ds(i * 128, 128)
        total = lo_f[rows, :] + tok[own, :].astype(F32)
        for j in range(3):
            total = total + lo_r[j, own, :].astype(F32)
        lo_out[own, :] = total.astype(BF16)

    gb_z = grad_z(gb, 1, gb_x)
    grad_end(0, ga_c)
    for other in range(2):
        @pl.when(jnp.logical_or(z // 2 != y, a != other))
        def _():
            remote(
                ofr.at[other], ofr.at[other], at_ctx(1), go_end_first, go_end_recv + other
            ).wait_recv()

        go_out[:, other * 256 : (other + 1) * 256] = ofr[other]
    gb_c = grad_ctx(1, gb_z)

    arrive(dx_y)
    for i, rows in enumerate((early, late)):
        own = pl.ds(i * 128, 128)
        total = dx_f[rows, :]
        for j in range(3):
            total = total + dx_r[j, own, :].astype(F32)
        xn, r = normed(own)
        first_mean = jnp.mean(total, axis=-1, keepdims=True)
        second_mean = jnp.mean(total * xn, axis=-1, keepdims=True)
        total = r * (total - first_mean - xn * second_mean) + cot[own, :].astype(F32)
        dt_out[own, :] = total.astype(BF16)
    grad_end(1, gb_c)

    for copy in started:
        copy.wait_send()

    @pl.when(owner)
    def _():
        for s in range(1, NZ):
            wo_copy(s).wait_send()
        for s in range(1, 8):
            go_end(s).wait_send()

    for j in range(2):
        @pl.when(z != 2 * y + j)
        def _():
            go_copy(j).wait_send()


N_SEMS = 136
SCRATCH = dict(
    xa=((1024, D), BF16), ca=((1024, D), BF16), xt=((D, 1024), BF16),
    w5=((NZ, 2, 2, 16, D), BF16), wo5=((2, 2, 2, 16, D), BF16), wgt=((128, D), BF16),
    kv=((2, 1024, 256), BF16), kvt=((2, 256, 1024), BF16), qs=((1024, 128), BF16),
    slope=((1024, 384), F32), gate_t=((128, 1024), F32), slope_gt=((128, 1024), F32),
    dg_t=((128, 1024), F32), dz_t=((128, 1024), F32),
    at=((18, 256, 256), BF16), sl=((18, 256, 256), F32), mixed_t=((128, 1024), F32),
    stats=((4, 8, 1024), F32), dm_t=((128, 1024), BF16), z_t=((128, 1024), BF16),
    dq_t=((128, 1024), F32), dkv_own=((1024, 256), F32), dkv_far=((1024, 256), F32),
    dkv_s=((1024, 256), BF16), dkv_r=((1024, 256), BF16),
    lo_f=((1024, D), F32), lo_s=((1024, D), BF16), lo_r=((3, 256, D), BF16),
    dpre=((1024, D), BF16), dx_f=((1024, D), F32), dx_s=((1024, D), BF16), dx_r=((3, 256, D), BF16),
    ga=((NZ, 2, 2, 16, 256), F32), gb=((NZ, 2, 2, 16, 256), F32),
    s1=((2, NZ, 2, 16, 256), BF16), r1=((2, NZ, 2, 16, 256), BF16),
    s2=((2, 4, NZ, 16, 128), BF16), r2=((2, 3, NZ, 16, 128), BF16), tot=((2, NZ, 16, 128), F32),
    s3=((2, NZ, 16, 128), BF16), r3=((2, NZ - 1, 16, 128), BF16), fr=((2, 8, 16, 128), F32),
    go=((2, 2, 2, 16, D), F32), os1=((2, 2, 16, D), BF16), or1=((2, 2, 16, D), BF16),
    os2=((4, 2, 16, 256), BF16), or2=((3, 2, 16, 256), BF16), otot=((2, 16, 256), F32),
    os3=((2, 16, 256), BF16), or3=((NZ, 16, 256), BF16), ofr=((2, 16, 256), F32),
)


def body(tokens, seq_lengths, w_in, w_out, cotangent):
    vmem = pl.BlockSpec(memory_space=pltpu.VMEM)
    return pl.pallas_call(
        kernel,
        name="hstu",
        out_shape=(
            jax.ShapeDtypeStruct((256, D), BF16),
            jax.ShapeDtypeStruct((256, D), BF16),
            jax.ShapeDtypeStruct((16, 4 * D), F32),
            jax.ShapeDtypeStruct((16, D), F32),
        ),
        in_specs=[vmem, pl.BlockSpec(memory_space=pltpu.SMEM), vmem, vmem, vmem],
        out_specs=(vmem, vmem, vmem, vmem),
        scratch_shapes=[pltpu.VMEM(*spec) for spec in SCRATCH.values()]
        + [pltpu.SemaphoreType.DMA((N_SEMS,)), pltpu.SemaphoreType.DMA((N_SEMS,))],
        compiler_params=pltpu.CompilerParams(
            collective_id=0, has_side_effects=True, vmem_limit_bytes=56 * 2**20
        ),
    )(tokens, seq_lengths, w_in, w_out, cotangent)


def solution(mesh):
    return jax.shard_map(
        body,
        mesh=mesh,
        in_specs=(
            P(("dp", "ctx"), None),
            P("dp", None),
            P("dp", None),
            P("dp", None),
            P(("dp", "ctx"), None),
        ),
        out_specs=(P(("dp", "ctx"), None), P(("dp", "ctx"), None), P("dp", None), P("dp", None)),
        check_vma=False,
    )
```

time: 703 us -> 92.8 us (0.13)
  waiting for transfers between devices: 548 us -> 0 us
  Pallas kernels: 0 us -> 87.4 us
  matrix products: 53.1 us -> 0 us
  blocking collectives: 38.6 us -> 0 us
  other arithmetic: 24 us -> 0 us
  local copies, waits for them, and re-layouts: 19.1 us -> 4.08 us
  between operations: 14 us -> 0.65 us
    ppermute x22 -> x0, waiting for transfers between devices: 316 us -> none  [shifted(): lax.ppermute(shard, axis, [(i, (i + by) % count) for i in range(count)])]
    reduce_scatter x1 -> x0, waiting for transfers between devices: 119 us -> none  [body(): lax.psum_scatter(jnp.concatenate([in_term, out_term], axis=1), 'dp', scat...]
    pallas_call x0 -> x1, Pallas kernels: none -> 87.4 us  [body(): pl.pallas_call(kernel, name='hstu', out_shape=(jax.ShapeDtypeStruct((256,...]
    psum x1 -> x0, waiting for transfers between devices: 84.3 us -> none  [body(): owner_rows = lax.psum(owner_rows, 'ctx')]
    dot_general x54 -> x0, matrix products: 53.1 us -> none  [the longest x8 12.7 us: backward_block(): jnp.einsum('ihd,jhd->hij', d_mixed_heads, split_heads(value_rows), prefer...]
    all_gather x1 -> x0, blocking collectives: 38.6 us -> none  [body(): lax.all_gather(w_out, 'dp', axis=0, tiled=True)]
    all_gather x1 -> x0, waiting for transfers between devices: 27.4 us -> none  [body(): w_whole = lax.all_gather(w_in, 'dp', axis=0, tiled=True)]
    while x18 -> x0, local copies, waits for them, and re-layouts: 9.94 us -> none
  transfers between devices with their start and end apart: 25 -> 0, of which waited for: 25 -> 0; matrix products, arithmetic and copies ran while one was open for 6% -> 0% of each run, Pallas kernels for 0% -> 0%
where the time goes in v1:
time: 92.8 us; the launch traced here: 92.1 us
  Pallas kernels  87.4 us (94%)
  local copies, waits for them, and re-layouts  4.08 us (4%)
    pallas_call x1, Pallas kernels, body(): pl.pallas_call(kernel, name='hstu', out_shape=(jax.ShapeDtypeStruct((256,...  87.4 us
    unnamed x10, local copies, waits for them, and re-layouts  4.08 us

profile of v1, /device:TPU:4, one launch (start us, length us, event | category | flops | bytes accessed | tf_op | source)
XLA Modules:
  0.0 92.1 jit_solution(249163232616236601)
XLA Ops:
  0.6 87.4 %hstu.1 = (bf16[256,512]{1,0:T(8,128)(2,1)}, bf16[256,512]{1,0:T(8,128)(2,1)}, f32[16,2048]{1,0:T(8,128)}, f32[16,512]{1,0:T(8,128)}) custom-call(bf16[256,512]{1,0:T(8,128)(2,1)} %tok.1, s32[1,2]{1,0:T(1,128)} %seq.1, bf16[16,2048]{1,0:T(8,128)(2,1)} %win.1, bf16[16,512]{1,0:T(8,128)(2,1)} %wout.1, bf16[256,512]{1,0:T(8,128)(2,1)} %cot.1), custom_call_target="tpu_custom_call" | custom-call | tf_op jit(solution)/shard_map/hstu/pallas_call | solution.py:513
  88.0 0.0 copy-start
  88.0 1.7 %copy.13 = bf16[256,512]{1,0:T(8,128)(2,1)} copy(bf16[256,512]{1,0:T(8,128)(2,1)} %get-tuple-element.8) | data formatting | bytes 524288
  89.7 0.0 copy-done
  89.7 0.0 copy-start.1
  89.7 0.7 copy.14
  90.4 0.3 copy-done.1
  90.7 0.0 copy-start.2
  90.7 0.7 copy.15
  91.4 0.1 copy-done.2
  91.5 0.6 copy.16
Async XLA Ops:
  88.0 1.7 %copy-start = (bf16[256,512]{1,0:T(8,128)(2,1)S(1)}, bf16[256,512]{1,0:T(8,128)(2,1)}, u32[]{:S(2)}) copy-start(bf16[256,512]{1,0:T(8,128)(2,1)} %get-tuple-element.9) | copy-start | bytes 786436
  89.7 1.0 %copy-start.1 = (f32[16,2048]{1,0:T(8,128)S(1)}, f32[16,2048]{1,0:T(8,128)}, u32[]{:S(2)}) copy-start(f32[16,2048]{1,0:T(8,128)} %get-tuple-element.10) | copy-start | bytes 393220
  90.7 0.8 copy-start.2

commit v2 on v1

v2 whole, which is shorter than its diff:
```python
import math

import jax
import jax.numpy as jnp
from jax import lax
from jax.experimental import pallas as pl
from jax.experimental.pallas import tpu as pltpu
from jax.sharding import PartitionSpec as P

MESH = pl.DeviceIdType.MESH
F32 = jnp.float32
BF16 = jnp.bfloat16
EPS = 1e-05
NZ = 8
D = 512
H = 128
SCALE = 1.0 / math.sqrt(H)
NN = (((1,), (0,)), ((), ()))
NT = (((1,), (1,)), ((), ()))
BASE = (0, 4, 7, 9)


def dot(lhs, rhs, dims=NN):
    return lax.dot_general(lhs, rhs, dims, preferred_element_type=F32)


def sigmoid(v):
    return 0.5 * jnp.tanh(0.5 * v) + 0.5


def kernel(
    tok, seq, win, wout, cot, lo_hbm, dt_hbm, gi_hbm, go_hbm,
    xa, ca, xt, w5, wo5, wgt, kv, kvt, qs, slope, gate_t, slope_gt, dg_t, dz_t,
    at, sl, at_far, sl_far, mixed_t, stats, dm_t, z_t, z_r, g_r, dq_t, dkv_own, dkv_far, dkv_s, dkv_r,
    dpre, dx_f, dx_s, dx_r,
    ga, gb, s1, r1, s2, r2, tot, s3, r3, fr,
    go, os1, or1, os2, or2, otot, os3, or3, ofr,
    lo_out, dt_out, gi_out, go_out,
    ssem, rsem, osem,
):
    dp = lax.axis_index("dp")
    cx = lax.axis_index("ctx")
    z, xl, k = dp // 4, (dp // 2) % 2, dp % 2
    a, y = cx // 4, cx % 4
    x = a * 2 + xl

    def at_y(s):
        return {"dp": dp, "ctx": a * 4 + (y + s) % 4}

    def at_x(s):
        there = (x + s) % 4
        return {"dp": z * 4 + (there % 2) * 2 + k, "ctx": (there // 2) * 4 + y}

    def at_z(s):
        return {"dp": ((z + s) % NZ) * 4 + xl * 2 + k, "ctx": cx}

    def at_zabs(there):
        return {"dp": there * 4 + xl * 2 + k, "ctx": cx}

    def at_ctx(s):
        return {"dp": dp, "ctx": (cx + s) % 8}

    core = {"dp": z * 4 + xl * 2 + (1 - k), "ctx": cx}
    xl_mate = {"dp": z * 4 + (1 - xl) * 2 + k, "ctx": cx}
    diagonal_mate = {"dp": z * 4 + (1 - xl) * 2 + (1 - k), "ctx": cx}
    far = {"dp": dp, "ctx": (1 - a) * 4 + y}

    peers = [core, diagonal_mate, at_x(1), at_x(3)]
    peers += [at_z(s) for s in range(1, NZ)]
    peers += [at_ctx(s) for s in range(1, 8)]
    barrier = pltpu.get_barrier_semaphore()
    for peer in peers:
        pl.semaphore_signal(barrier, inc=1, device_id=peer, device_id_type=MESH)

    counter = [0]
    started = []

    def sems(n=1):
        first = counter[0]
        counter[0] += n
        return first

    def remote(src, dst, peer, s_index, r_index):
        return pltpu.make_async_remote_copy(
            src_ref=src, dst_ref=dst, send_sem=ssem.at[s_index], recv_sem=rsem.at[r_index],
            device_id=peer, device_id_type=MESH,
        )

    def send(src, dst, peer):
        i = sems()
        copy = remote(src, dst, peer, i, i)
        copy.start()
        started.append(copy)
        return copy

    def arrive(copies):
        for copy in copies:
            copy.wait_recv()

    early = pl.ds(pl.multiple_of(y * 128, 128), 128)
    late = pl.ds(pl.multiple_of((7 - y) * 128, 128), 128)

    def slots(s):
        there = (y + s) % 4
        return (
            pl.ds(pl.multiple_of(there * 128, 128), 128),
            pl.ds(pl.multiple_of((7 - there) * 128, 128), 128),
        )

    for part, block in enumerate((2, 3, 0, 1)):
        w5[z, xl, k, :, part * 128 : (part + 1) * 128] = win[
            :, pl.ds(pl.multiple_of(block * D + y * 128, 128), 128)
        ]
    wo5[z, xl, k] = wout[...]
    owner = z // 2 == y

    def normed(rows):
        v = tok[rows, :].astype(F32)
        centre = v - jnp.mean(v, axis=-1, keepdims=True)
        spread = lax.rsqrt(jnp.mean(centre * centre, axis=-1, keepdims=True) + EPS)
        return centre * spread, spread

    xa[early, :] = normed(pl.ds(0, 128))[0].astype(BF16)
    xa[late, :] = normed(pl.ds(128, 128))[0].astype(BF16)
    ca[early, :] = cot[0:128, :]
    ca[late, :] = cot[128:256, :]

    pl.semaphore_wait(barrier, len(peers))

    front, back = pl.ds(0, 256), pl.ds(256, 256)

    z_order = (4, 3, 5, 2, 6, 1, 7)

    def along_z(ref, *columns):
        part = ref.at[z, xl, k, :, *columns]
        return [send(part, part, at_z(s)) for s in z_order]

    def along_x(ref, *columns):
        part = ref.at[:, xl, k, :, *columns]
        return send(part, part, xl_mate)

    def to_core(ref, *columns):
        part = ref.at[:, :, k, :, *columns]
        return send(part, part, core)

    def onward(there):
        part = w5.at[there, xl, k, :, front]
        return [send(part, part, mate) for mate in (xl_mate, diagonal_mate, core)]

    order = (0, 1, 3, 2)
    kv_z = along_z(w5, front)
    kv_w = onward(z)
    x_y = {}
    for s in order[1:]:
        x_y[s] = [send(xa.at[early], xa.at[early], at_y(s)), send(xa.at[late], xa.at[late], at_y(s))]
    gq_z = along_z(w5, back)
    for s in (1, 7, 2, 6, 3, 5, 4):
        arrive([kv_z[z_order.index(s)]])
        kv_w += onward((z - s) % NZ)
    wo_z = along_z(wo5)
    arrive(gq_z)
    gq_w = along_x(w5, back)
    arrive(kv_w)

    def place_of(s):
        return (y - s) % 4

    def rows_of(block):
        return (
            pl.ds(pl.multiple_of(block * 128, 128), 128),
            pl.ds(pl.multiple_of((7 - block) * 128, 128), 128),
        )

    def kv_late(rows, index):
        return remote(kv.at[a, rows], kv.at[a, rows], far, index, index)

    late_first = sems(4)
    kv_x = []
    w_kv = w5[:, :, :, :, 0:256].reshape(D, 256)
    for i, s in enumerate(order):
        if s:
            arrive(x_y[s])
        if i == 3:
            c_y = []
            for t in order[1:]:
                c_y.append(send(ca.at[early], ca.at[early], at_y(t)))
                c_y.append(send(ca.at[late], ca.at[late], at_y(t)))
        first, last = rows_of(place_of(s))
        for rows in (first, last):
            pre = dot(xa[rows, :], w_kv)
            sig = sigmoid(pre)
            act = pre * sig
            kv[a, rows, :] = act.astype(BF16)
            slope[rows, 128:384] = sig + act * (1.0 - sig)
        kv_x.append(send(kv.at[a, first], kv.at[a, first], far))

        @pl.when(a == 1)
        def _():
            kv_late(last, late_first + i).start()

    arrive([gq_w])
    gq_w = to_core(w5, back)
    arrive(wo_z)
    wo_w = along_x(wo5)
    arrive([gq_w])
    wgt[...] = w5[:, :, :, :, 256:384].reshape(D, 128).T
    for i in range(4):
        rows = pl.ds(i * 256, 256)
        pre = dot(xa[rows, :], w5[:, :, :, :, 384:512].reshape(D, 128))
        sig = sigmoid(pre)
        act = pre * sig
        qs[rows, :] = act.astype(BF16)
        slope[rows, 0:128] = sig + act * (1.0 - sig)
        pre = dot(wgt[...], xa[rows, :], NT)
        sig = sigmoid(pre)
        act = pre * sig
        gate_t[:, rows] = act.astype(BF16).astype(F32)
        slope_gt[:, rows] = sig + act * (1.0 - sig)
        kvt[a, :, rows] = kv[a, rows, :].T
        xt[:, rows] = xa[rows, :].T
    arrive([wo_w])
    wo_w = to_core(wo5)

    mixed_t[...] = jnp.zeros_like(mixed_t)
    border = seq[0, 0]

    def tile(i):
        return pl.ds(pl.multiple_of(i * 256, 256), 256)

    def place(half, i):
        return i * 256 + half * 512 + (1 - half) * 1024 * (i // 2)

    def attend(half, kt, qt, index, diagonal):
        scores = dot(kv[half, tile(kt), 0:128], qs[tile(qt), :], NT)
        key_at = lax.broadcasted_iota(jnp.int32, (256, 256), 0) + place(half, kt)
        query_at = lax.broadcasted_iota(jnp.int32, (1, 256), 1) + place(a, qt)
        least = jnp.where(query_at >= border, border, 0)
        allowed = key_at >= least
        if diagonal:
            allowed = allowed & (key_at <= query_at)
        s = scores * SCALE
        sig = jnp.where(allowed, sigmoid(s), 0.0)
        act = s * sig
        act_b = act.astype(BF16)
        at[index] = act_b
        sl[index] = sig + act * (1.0 - sig)
        mixed_t[:, tile(qt)] += dot(kvt[half, 128:256, tile(kt)], act_b)

    for kt in range(4):
        for qt in range(kt, 4):
            attend(a, kt, qt, BASE[kt] + qt - kt, qt == kt)

    def far_tile(block, j):
        key_slot = block + (1 - a) * j * (7 - 2 * block)
        query_first = (1 - a + a * j) * 512
        return (
            key_slot,
            pl.ds(pl.multiple_of(key_slot * 128, 128), 128),
            pl.ds(pl.multiple_of(query_first, 512), 512),
            query_first,
        )

    def slot_place(half, slot):
        return slot * 128 + half * 512 + (1 - half) * 1024 * (slot // 4)

    for i, s in enumerate(order):
        block = place_of(s)
        first, last = rows_of(block)
        arrive([kv_x[i]])
        kvt[1 - a, :, first] = kv[1 - a, first, :].T

        @pl.when(a == 0)
        def _():
            kv_late(last, late_first + i).wait_recv()
            kvt[1, :, last] = kv[1, last, :].T

        for j in range(2):
            slot, keys, queries, query_first = far_tile(block, j)
            s_t = dot(kv[1 - a, keys, 0:128], qs[queries, :], NT) * SCALE
            key_at = lax.broadcasted_iota(jnp.int32, (128, 512), 0) + slot_place(1 - a, slot)
            query_at = lax.broadcasted_iota(jnp.int32, (1, 512), 1) + slot_place(a, query_first // 128)
            sig = jnp.where(key_at >= jnp.where(query_at >= border, border, 0), sigmoid(s_t), 0.0)
            act = s_t * sig
            act_b = act.astype(BF16)
            at_far[2 * i + j] = act_b
            sl_far[2 * i + j] = sig + act * (1.0 - sig)
            mixed_t[:, queries] += dot(kvt[1 - a, 128:256, keys], act_b)

    arrive(c_y)
    arrive([wo_w])
    head = pl.ds(pl.multiple_of(y * 2, 2), 2)
    for i in range(4):
        rows = pl.ds(i * 256, 256)
        part = dot(wo5[head].reshape(128, D), ca[rows, :], NT)
        dg_t[:, rows] = part
        dz_t[:, rows] = part * gate_t[:, rows]
    mixed = mixed_t[...]
    mean_h = jnp.mean(mixed, axis=0, keepdims=True)
    centred = mixed - mean_h
    dz = dz_t[...]
    stats[y, 0:1, :] = mean_h
    stats[y, 1:2, :] = jnp.sum(centred * centred, axis=0, keepdims=True)
    stats[y, 2:3, :] = jnp.sum(dz, axis=0, keepdims=True)
    stats[y, 3:4, :] = jnp.sum(dz * centred, axis=0, keepdims=True)
    stats[y, 4:8, :] = jnp.zeros((4, 1024), F32)
    arrive([send(stats.at[y], stats.at[y], at_y(s)) for s in (1, 2, 3)])
    means = [stats[j, 0:1, :] for j in range(4)]
    mean = (means[0] + means[1] + means[2] + means[3]) * 0.25
    second = jnp.zeros((1, 1024), F32)
    first_dz = jnp.zeros((1, 1024), F32)
    second_dz = jnp.zeros((1, 1024), F32)
    for j in range(4):
        off = means[j] - mean
        second += stats[j, 1:2, :] + 128.0 * off * off
        first_dz += stats[j, 2:3, :]
        second_dz += stats[j, 3:4, :] + off * stats[j, 2:3, :]
    spread = lax.rsqrt(second * (1.0 / D) + EPS)
    first_dz = first_dz * (1.0 / D)
    second_dz = second_dz * (1.0 / D) * spread
    for i in range(4):
        rows = pl.ds(i * 256, 256)
        r = spread[:, i * 256 : (i + 1) * 256]
        zn = (mixed_t[:, rows] - mean[:, i * 256 : (i + 1) * 256]) * r
        z_t[:, rows] = (zn * gate_t[:, rows]).astype(BF16)
        dm_t[:, rows] = (
            r * (
                dz_t[:, rows] - first_dz[:, i * 256 : (i + 1) * 256]
                - zn * second_dz[:, i * 256 : (i + 1) * 256]
            )
        ).astype(BF16)
        dpre[rows, 256:384] = (dg_t[:, rows] * zn * slope_gt[:, rows]).astype(BF16).T

    dq_t[...] = jnp.zeros_like(dq_t)
    dkv_own[...] = jnp.zeros_like(dkv_own)
    dkv_far[...] = jnp.zeros_like(dkv_far)

    def attend_back(half, kt, qt, index, grads):
        d_attn = dot(kv[half, tile(kt), 128:256], dm_t[:, tile(qt)])
        ds = (d_attn * sl[index]).astype(BF16)
        grads[tile(kt), 128:256] += dot(at[index], dm_t[:, tile(qt)], NT)
        grads[tile(kt), 0:128] += dot(ds, qs[tile(qt), :])
        dq_t[:, tile(qt)] += dot(kvt[half, 0:128, tile(kt)], ds)

    def dkv_late(rows, index):
        return remote(dkv_s.at[rows], dkv_r.at[rows], far, index, index)

    @pl.when(a == 0)
    def _():
        dkv_r[512:1024, :] = jnp.zeros((512, 256), BF16)

    back_order = (2, 1, 3, 0)
    dkv_late_first = sems(4)
    dkv_x = []
    for i, s in enumerate(back_order):
        block = (y + s) % 4
        first, last = rows_of(block)
        index = 2 * order.index((4 - s) % 4)
        for j in range(2):
            slot, keys, queries, _ = far_tile(block, j)
            d_attn = dot(kv[1 - a, keys, 128:256], dm_t[:, queries])
            ds = (d_attn * sl_far[index + j]).astype(BF16)
            dkv_far[keys, 128:256] += dot(at_far[index + j], dm_t[:, queries], NT)
            dkv_far[keys, 0:128] += dot(ds, qs[queries, :])
            dq_t[:, queries] += dot(kvt[1 - a, 0:128, keys], ds)
        dkv_s[first, :] = dkv_far[first, :].astype(BF16)
        dkv_x.append(send(dkv_s.at[first], dkv_r.at[first], far))

        @pl.when(a == 0)
        def _():
            dkv_s[last, :] = dkv_far[last, :].astype(BF16)
            dkv_late(last, dkv_late_first + i).start()

    z_r[...] = z_t[...].T
    g_r[y, 0:128, :] = z_r[early, :]
    g_r[y, 128:256, :] = z_r[late, :]
    g_y = []
    for s in order[1:]:
        to_early, to_late = slots(s)
        g_y.append(send(z_r.at[to_early], g_r.at[y, pl.ds(0, 128)], at_y(s)))
        g_y.append(send(z_r.at[to_late], g_r.at[y, pl.ds(128, 128)], at_y(s)))
    for kt in range(4):
        for qt in range(kt, 4):
            attend_back(a, kt, qt, BASE[kt] + qt - kt, dkv_own)

    for i in range(4):
        rows = pl.ds(i * 256, 256)
        dpre[rows, 384:512] = ((dq_t[:, rows] * SCALE).T * slope[rows, 0:128]).astype(BF16)

    def grad_start(grads, first_column, n):
        for i in range(2):
            rows = pl.ds(i * 256, 256)
            part = dot(xt[rows, :], dpre[:, first_column : first_column + 256])
            grads[i * 4 : (i + 1) * 4] = part.reshape(4, 2, 2, 16, 256)
        s1[n] = grads[:, :, 1 - k].astype(BF16)
        return send(s1.at[n], r1.at[n], core)

    def grad_x(grads, n, copy):
        arrive([copy])
        grads[:, :, k] = grads[:, :, k] + r1[n].astype(F32)
        for there in range(4):
            s2[n, there] = grads[
                :, there % 2, k, :, (there // 2) * 128 : (there // 2 + 1) * 128
            ].astype(BF16)
        return [send(s2.at[n, (x + s) % 4], r2.at[n, s - 1], at_x(s)) for s in (1, 2, 3)]

    def grad_z(grads, n, copies):
        arrive(copies)
        total = grads[:, xl, k, :, pl.ds(pl.multiple_of(a * 128, 128), 128)]
        total = total + r2[n, 0].astype(F32) + r2[n, 1].astype(F32) + r2[n, 2].astype(F32)
        tot[n] = total
        s3[n] = total.astype(BF16)
        return [send(s3.at[n, (z + s) % NZ], r3.at[n, s - 1], at_z(s)) for s in range(1, NZ)]

    def grad_ctx(n, copies):
        arrive(copies)
        total = tot[n, z]
        for s in range(NZ - 1):
            total = total + r3[n, s].astype(F32)
        fr[n, cx] = total
        return [send(fr.at[n, cx], fr.at[n, cx], at_ctx(s)) for s in range(1, 8)]

    def grad_end(n, copies):
        arrive(copies)
        for c in range(8):
            first = (n * 2 + c // 4) * D + (c % 4) * 128
            gi_out[:, first : first + 128] = fr[n, c]

    go_end_first = sems(8)
    go_end_recv = sems(2)

    def go_end(s):
        return remote(ofr.at[a], ofr.at[a], at_ctx(s), go_end_first + s, go_end_recv + a)


    dx_y = []
    w_t = w5[...].reshape(D, D)
    for i, s in enumerate(back_order):
        first, last = rows_of((y + s) % 4)
        arrive([dkv_x[i]])

        @pl.when(a == 1)
        def _():
            dkv_late(last, dkv_late_first + i).wait_recv()

        for half, rows in enumerate((first, last)):
            both = dkv_own[rows, :] + dkv_r[rows, :].astype(F32)
            dpre[rows, 0:128] = (both[:, 0:128] * SCALE * slope[rows, 128:256]).astype(BF16)
            dpre[rows, 128:256] = (both[:, 128:256] * slope[rows, 256:384]).astype(BF16)
            if s:
                dx_s[rows, :] = dot(dpre[rows, :], w_t, NT).astype(BF16)
                own = pl.ds(half * 128, 128)
                dx_y.append(send(dx_s.at[rows], dx_r.at[s - 1, own], at_y(s)))
        if i == 1:
            go[...] = dot(z_t[...], ca[...]).reshape(2, 2, 2, 16, D)
            os1[...] = go[:, :, 1 - k].astype(BF16)
            go_k = send(os1, or1, core)
        if i == 2:
            ga_k = grad_start(ga, 256, 0)
    gb_k = grad_start(gb, 0, 1)
    for half, rows in enumerate((early, late)):
        dx_f[half * 128 : (half + 1) * 128, :] = dot(dpre[rows, :], w_t, NT)
    arrive([go_k])
    go[:, :, k] = go[:, :, k] + or1[...].astype(F32)
    for there in range(4):
        os2[there] = go[:, there % 2, k, :, (there // 2) * 256 : (there // 2 + 1) * 256].astype(BF16)
    go_x = [send(os2.at[(x + s) % 4], or2.at[s - 1], at_x(s)) for s in (1, 2, 3)]
    ga_x = grad_x(ga, 0, ga_k)
    gb_x = grad_x(gb, 1, gb_k)
    arrive(go_x)
    total = go[:, xl, k, :, pl.ds(pl.multiple_of(a * 256, 256), 256)]
    total = total + or2[0].astype(F32) + or2[1].astype(F32) + or2[2].astype(F32)
    otot[...] = total
    os3[...] = total.astype(BF16)
    go_first = sems(NZ)
    go_sent = sems(2)

    def go_copy(j):
        return remote(os3.at[j], or3.at[z], at_zabs(2 * y + j), go_sent + j, go_first + z)

    for j in range(2):
        @pl.when(z != 2 * y + j)
        def _():
            go_copy(j).start()

    arrive(g_y)
    for own in (pl.ds(0, 128), pl.ds(128, 128)):
        total = tok[own, :].astype(F32)
        for h in range(4):
            total = total + dot(g_r[h, own, :], wo5[2 * h : 2 * h + 2].reshape(128, D))
        lo_out[own, :] = total.astype(BF16)
    to_hbm = [pltpu.make_async_copy(lo_out, lo_hbm, osem.at[0])]
    to_hbm[0].start()
    ga_z = grad_z(ga, 0, ga_x)
    gb_z = grad_z(gb, 1, gb_x)
    @pl.when(owner)
    def _():
        final = otot[z % 2]
        for s in range(1, NZ):
            source = (z + s) % NZ
            remote(
                os3.at[0], or3.at[source], at_z(s), go_sent, go_first + source
            ).wait_recv()
            final = final + or3[source].astype(F32)
        ofr[a] = final
        for s in range(1, 8):
            go_end(s).start()

    ga_c = grad_ctx(0, ga_z)
    arrive(dx_y)
    for i, rows in enumerate((early, late)):
        own = pl.ds(i * 128, 128)
        total = dx_f[own, :]
        for j in range(3):
            total = total + dx_r[j, own, :].astype(F32)
        xn, r = normed(own)
        first_mean = jnp.mean(total, axis=-1, keepdims=True)
        second_mean = jnp.mean(total * xn, axis=-1, keepdims=True)
        total = r * (total - first_mean - xn * second_mean) + cot[own, :].astype(F32)
        dt_out[own, :] = total.astype(BF16)
    to_hbm.append(pltpu.make_async_copy(dt_out, dt_hbm, osem.at[2]))
    to_hbm[-1].start()
    gb_c = grad_ctx(1, gb_z)
    for other in range(2):
        @pl.when(jnp.logical_or(z // 2 != y, a != other))
        def _():
            remote(
                ofr.at[other], ofr.at[other], at_ctx(1), go_end_first, go_end_recv + other
            ).wait_recv()

        go_out[:, other * 256 : (other + 1) * 256] = ofr[other]
    to_hbm.append(pltpu.make_async_copy(go_out, go_hbm, osem.at[1]))
    to_hbm[-1].start()
    grad_end(0, ga_c)
    grad_end(1, gb_c)
    to_hbm.append(pltpu.make_async_copy(gi_out, gi_hbm, osem.at[3]))
    to_hbm[-1].start()

    for copy in started:
        copy.wait_send()

    @pl.when(a == 1)
    def _():
        for i, s in enumerate(order):
            kv_late(rows_of(place_of(s))[1], late_first + i).wait_send()

    @pl.when(a == 0)
    def _():
        for i, s in enumerate(back_order):
            dkv_late(rows_of((y + s) % 4)[1], dkv_late_first + i).wait_send()

    @pl.when(owner)
    def _():
        for s in range(1, 8):
            go_end(s).wait_send()

    for j in range(2):
        @pl.when(z != 2 * y + j)
        def _():
            go_copy(j).wait_send()

    for copy in to_hbm:
        copy.wait()


N_SEMS = 200
SCRATCH = dict(
    xa=((1024, D), BF16), ca=((1024, D), BF16), xt=((D, 1024), BF16),
    w5=((NZ, 2, 2, 16, D), BF16), wo5=((NZ, 2, 2, 16, D), BF16), wgt=((128, D), BF16),
    kv=((2, 1024, 256), BF16), kvt=((2, 256, 1024), BF16), qs=((1024, 128), BF16),
    slope=((1024, 384), F32), gate_t=((128, 1024), F32), slope_gt=((128, 1024), F32),
    dg_t=((128, 1024), F32), dz_t=((128, 1024), F32),
    at=((10, 256, 256), BF16), sl=((10, 256, 256), F32),
    at_far=((8, 128, 512), BF16), sl_far=((8, 128, 512), F32), mixed_t=((128, 1024), F32),
    stats=((4, 8, 1024), F32), dm_t=((128, 1024), BF16), z_t=((128, 1024), BF16),
    z_r=((1024, 128), BF16), g_r=((4, 256, 128), BF16),
    dq_t=((128, 1024), F32), dkv_own=((1024, 256), F32), dkv_far=((1024, 256), F32),
    dkv_s=((1024, 256), BF16), dkv_r=((1024, 256), BF16),
    dpre=((1024, D), BF16), dx_f=((256, D), F32), dx_s=((1024, D), BF16), dx_r=((3, 256, D), BF16),
    ga=((NZ, 2, 2, 16, 256), F32), gb=((NZ, 2, 2, 16, 256), F32),
    s1=((2, NZ, 2, 16, 256), BF16), r1=((2, NZ, 2, 16, 256), BF16),
    s2=((2, 4, NZ, 16, 128), BF16), r2=((2, 3, NZ, 16, 128), BF16), tot=((2, NZ, 16, 128), F32),
    s3=((2, NZ, 16, 128), BF16), r3=((2, NZ - 1, 16, 128), BF16), fr=((2, 8, 16, 128), F32),
    go=((2, 2, 2, 16, D), F32), os1=((2, 2, 16, D), BF16), or1=((2, 2, 16, D), BF16),
    os2=((4, 2, 16, 256), BF16), or2=((3, 2, 16, 256), BF16), otot=((2, 16, 256), F32),
    os3=((2, 16, 256), BF16), or3=((NZ, 16, 256), BF16), ofr=((2, 16, 256), F32),
    lo_out=((256, D), BF16), dt_out=((256, D), BF16), gi_out=((16, 4 * D), F32), go_out=((16, D), F32),
)


def move(*refs):
    for source, target in zip(refs[:4], refs[4:]):
        target[...] = source[...]


def body(tokens, seq_lengths, w_in, w_out, cotangent):
    vmem = pl.BlockSpec(memory_space=pltpu.VMEM)
    anywhere = pl.BlockSpec(memory_space=pl.ANY)
    outs = (
        jax.ShapeDtypeStruct((256, D), BF16),
        jax.ShapeDtypeStruct((256, D), BF16),
        jax.ShapeDtypeStruct((16, 4 * D), F32),
        jax.ShapeDtypeStruct((16, D), F32),
    )
    results = pl.pallas_call(
        kernel,
        name="hstu",
        out_shape=outs,
        in_specs=[vmem, pl.BlockSpec(memory_space=pltpu.SMEM), vmem, vmem, vmem],
        out_specs=(anywhere,) * 4,
        scratch_shapes=[pltpu.VMEM(*spec) for spec in SCRATCH.values()]
        + [pltpu.SemaphoreType.DMA((n,)) for n in (N_SEMS, N_SEMS, 4)],
        compiler_params=pltpu.CompilerParams(
            collective_id=0, has_side_effects=True, vmem_limit_bytes=56 * 2**20
        ),
    )(tokens, seq_lengths, w_in, w_out, cotangent)
    return pl.pallas_call(
        move,
        name="move",
        out_shape=outs,
        in_specs=[vmem] * 4,
        out_specs=(vmem,) * 4,
    )(*results)


def solution(mesh):
    return jax.shard_map(
        body,
        mesh=mesh,
        in_specs=(
            P(("dp", "ctx"), None),
            P("dp", None),
            P("dp", None),
            P("dp", None),
            P(("dp", "ctx"), None),
        ),
        out_specs=(P(("dp", "ctx"), None), P(("dp", "ctx"), None), P("dp", None), P("dp", None)),
        check_vma=False,
    )
```

time: 92.8 us -> 76.3 us (0.82)
  Pallas kernels: 87.4 us -> 75.5 us
  local copies, waits for them, and re-layouts: 4.08 us -> 0 us
    pallas_call x1 -> x2, Pallas kernels: 87.4 us -> 75.5 us  [the longest x1 73.6 us: body(): pl.pallas_call(kernel, name='hstu', out_shape=outs, in_specs=[vmem, pl.Bl...]
    unnamed x10 -> x0, local copies, waits for them, and re-layouts: 4.08 us -> none
where the time goes in v2:
time: 76.3 us; the launch traced here: 76.2 us
  Pallas kernels  75.5 us (99%)
    pallas_call x1, Pallas kernels, body(): pl.pallas_call(kernel, name='hstu', out_shape=outs, in_specs=[vmem, pl.Bl...  73.6 us
    pallas_call x1, Pallas kernels, body(): pl.pallas_call(move, name='move', out_shape=outs, in_specs=[vmem] * 4, ou...  1.92 us

profile of v2, /device:TPU:4, one launch (start us, length us, event | category | flops | bytes accessed | tf_op | source)
XLA Modules:
  0.0 76.2 jit_solution(802173121289766064)
XLA Ops:
  0.6 73.6 %hstu.1 = (bf16[256,512]{1,0:T(8,128)(2,1)}, bf16[256,512]{1,0:T(8,128)(2,1)}, f32[16,2048]{1,0:T(8,128)}, f32[16,512]{1,0:T(8,128)}) custom-call(bf16[256,512]{1,0:T(8,128)(2,1)} %tok.1, s32[1,2]{1,0:T(1,128)} %seq.1, bf16[16,2048]{1,0:T(8,128)(2,1)} %win.1, bf16[16,512]{1,0:T(8,128)(2,1)} %wout.1, bf16[256,512]{1,0:T(8,128)(2,1)} %cot.1), custom_call_target="tpu_custom_call" | custom-call | tf_op jit(solution)/shard_map/hstu/pallas_call | solution.py:604
  74.2 1.9 %move.1 = (bf16[256,512]{1,0:T(8,128)(2,1)}, bf16[256,512]{1,0:T(8,128)(2,1)}, f32[16,2048]{1,0:T(8,128)}, f32[16,512]{1,0:T(8,128)}) custom-call(bf16[256,512]{1,0:T(8,128)(2,1)} %get-tuple-element.8.refs_0_, bf16[256,512]{1,0:T(8,128)(2,1)} %get-tuple-element.9.refs_1_, f32[16,2048]{1,0:T(8,128)} %get-tuple-element.10.refs_2_, ...), custom_call_target="tpu_custom_call" | custom-call | tf_op jit(solution)/shard_map/move/pallas_call | solution.py:616

commit v3 on v2

--- a/solution.py
+++ b/solution.py
@@ -180,7 +180,7 @@
     for i, s in enumerate(order):
         if s:
             arrive(x_y[s])
-        if i == 3:
+        if i == 1:
             c_y = []
             for t in order[1:]:
                 c_y.append(send(ca.at[early], ca.at[early], at_y(t)))
@@ -218,9 +218,6 @@
         slope_gt[:, rows] = sig + act * (1.0 - sig)
         kvt[a, :, rows] = kv[a, rows, :].T
         xt[:, rows] = xa[rows, :].T
-    arrive([wo_w])
-    wo_w = to_core(wo5)
-
     mixed_t[...] = jnp.zeros_like(mixed_t)
     border = seq[0, 0]
 
@@ -250,6 +247,9 @@
         for qt in range(kt, 4):
             attend(a, kt, qt, BASE[kt] + qt - kt, qt == kt)
 
+    arrive([wo_w])
+    wo_w = to_core(wo5)
+
     def far_tile(block, j):
         key_slot = block + (1 - a) * j * (7 - 2 * block)
         query_first = (1 - a + a * j) * 512
@@ -294,26 +294,32 @@
         part = dot(wo5[head].reshape(128, D), ca[rows, :], NT)
         dg_t[:, rows] = part
         dz_t[:, rows] = part * gate_t[:, rows]
+    def put_sums(row, sums):
+        stats[y, row : row + 1, :] = sums[:, 0:512]
+        stats[y, row + 4 : row + 5, :] = sums[:, 512:1024]
+
+    def sums_of(j, row):
+        return jnp.concatenate([stats[j, row : row + 1, :], stats[j, row + 4 : row + 5, :]], axis=1)
+
     mixed = mixed_t[...]
     mean_h = jnp.mean(mixed, axis=0, keepdims=True)
     centred = mixed - mean_h
     dz = dz_t[...]
-    stats[y, 0:1, :] = mean_h
-    stats[y, 1:2, :] = jnp.sum(centred * centred, axis=0, keepdims=True)
-    stats[y, 2:3, :] = jnp.sum(dz, axis=0, keepdims=True)
-    stats[y, 3:4, :] = jnp.sum(dz * centred, axis=0, keepdims=True)
-    stats[y, 4:8, :] = jnp.zeros((4, 1024), F32)
+    put_sums(0, mean_h)
+    put_sums(1, jnp.sum(centred * centred, axis=0, keepdims=True))
+    put_sums(2, jnp.sum(dz, axis=0, keepdims=True))
+    put_sums(3, jnp.sum(dz * centred, axis=0, keepdims=True))
     arrive([send(stats.at[y], stats.at[y], at_y(s)) for s in (1, 2, 3)])
-    means = [stats[j, 0:1, :] for j in range(4)]
+    means = [sums_of(j, 0) for j in range(4)]
     mean = (means[0] + means[1] + means[2] + means[3]) * 0.25
     second = jnp.zeros((1, 1024), F32)
     first_dz = jnp.zeros((1, 1024), F32)
     second_dz = jnp.zeros((1, 1024), F32)
     for j in range(4):
         off = means[j] - mean
-        second += stats[j, 1:2, :] + 128.0 * off * off
-        first_dz += stats[j, 2:3, :]
-        second_dz += stats[j, 3:4, :] + off * stats[j, 2:3, :]
+        second += sums_of(j, 1) + 128.0 * off * off
+        first_dz += sums_of(j, 2)
+        second_dz += sums_of(j, 3) + off * sums_of(j, 2)
     spread = lax.rsqrt(second * (1.0 / D) + EPS)
     first_dz = first_dz * (1.0 / D)
     second_dz = second_dz * (1.0 / D) * spread
@@ -409,7 +415,7 @@
         total = total + r2[n, 0].astype(F32) + r2[n, 1].astype(F32) + r2[n, 2].astype(F32)
         tot[n] = total
         s3[n] = total.astype(BF16)
-        return [send(s3.at[n, (z + s) % NZ], r3.at[n, s - 1], at_z(s)) for s in range(1, NZ)]
+        return [send(s3.at[n, (z + s) % NZ], r3.at[n, s - 1], at_z(s)) for s in z_order]
 
     def grad_ctx(n, copies):
         arrive(copies)
@@ -417,7 +423,7 @@
         for s in range(NZ - 1):
             total = total + r3[n, s].astype(F32)
         fr[n, cx] = total
-        return [send(fr.at[n, cx], fr.at[n, cx], at_ctx(s)) for s in range(1, 8)]
+        return [send(fr.at[n, cx], fr.at[n, cx], at_ctx(s)) for s in (6, 2, 5, 7, 3, 4, 1)]
 
     def grad_end(n, copies):
         arrive(copies)
@@ -571,7 +577,7 @@
     dg_t=((128, 1024), F32), dz_t=((128, 1024), F32),
     at=((10, 256, 256), BF16), sl=((10, 256, 256), F32),
     at_far=((8, 128, 512), BF16), sl_far=((8, 128, 512), F32), mixed_t=((128, 1024), F32),
-    stats=((4, 8, 1024), F32), dm_t=((128, 1024), BF16), z_t=((128, 1024), BF16),
+    stats=((4, 8, 512), F32), dm_t=((128, 1024), BF16), z_t=((128, 1024), BF16),
     z_r=((1024, 128), BF16), g_r=((4, 256, 128), BF16),
     dq_t=((128, 1024), F32), dkv_own=((1024, 256), F32), dkv_far=((1024, 256), F32),
     dkv_s=((1024, 256), BF16), dkv_r=((1024, 256), BF16),

time: 76.3 us -> 74.4 us (0.975)
  Pallas kernels: 75.5 us -> 73.6 us
    pallas_call x1, Pallas kernels: 73.6 us -> 71.7 us  [body(): pl.pallas_call(kernel, name='hstu', out_shape=outs, in_specs=[vmem, pl.Bl...]
where the time goes in v3:
time: 74.4 us; the launch traced here: 74.3 us
  Pallas kernels  73.6 us (99%)
    pallas_call x1, Pallas kernels, body(): pl.pallas_call(kernel, name='hstu', out_shape=outs, in_specs=[vmem, pl.Bl...  71.7 us
    pallas_call x1, Pallas kernels, body(): pl.pallas_call(move, name='move', out_shape=outs, in_specs=[vmem] * 4, ou...  1.92 us

profile of v3, /device:TPU:4, one launch (start us, length us, event | category | flops | bytes accessed | tf_op | source)
XLA Modules:
  0.0 74.3 jit_solution(10714404251697560522)
XLA Ops:
  0.6 71.7 %hstu.1 = (bf16[256,512]{1,0:T(8,128)(2,1)}, bf16[256,512]{1,0:T(8,128)(2,1)}, f32[16,2048]{1,0:T(8,128)}, f32[16,512]{1,0:T(8,128)}) custom-call(bf16[256,512]{1,0:T(8,128)(2,1)} %tok.1, s32[1,2]{1,0:T(1,128)} %seq.1, bf16[16,2048]{1,0:T(8,128)(2,1)} %win.1, bf16[16,512]{1,0:T(8,128)(2,1)} %wout.1, bf16[256,512]{1,0:T(8,128)(2,1)} %cot.1), custom_call_target="tpu_custom_call" | custom-call | tf_op jit(solution)/shard_map/hstu/pallas_call | solution.py:610
  72.4 1.9 %move.1 = (bf16[256,512]{1,0:T(8,128)(2,1)}, bf16[256,512]{1,0:T(8,128)(2,1)}, f32[16,2048]{1,0:T(8,128)}, f32[16,512]{1,0:T(8,128)}) custom-call(bf16[256,512]{1,0:T(8,128)(2,1)} %get-tuple-element.8.refs_0_, bf16[256,512]{1,0:T(8,128)(2,1)} %get-tuple-element.9.refs_1_, f32[16,2048]{1,0:T(8,128)} %get-tuple-element.10.refs_2_, ...), custom_call_target="tpu_custom_call" | custom-call | tf_op jit(solution)/shard_map/move/pallas_call | solution.py:622

commit v4 on v3

--- a/solution.py
+++ b/solution.py
@@ -334,7 +334,7 @@
                 - zn * second_dz[:, i * 256 : (i + 1) * 256]
             )
         ).astype(BF16)
-        dpre[rows, 256:384] = (dg_t[:, rows] * zn * slope_gt[:, rows]).astype(BF16).T
+        dg_t[:, rows] = dg_t[:, rows] * zn
 
     dq_t[...] = jnp.zeros_like(dq_t)
     dkv_own[...] = jnp.zeros_like(dkv_own)
@@ -384,6 +384,10 @@
         to_early, to_late = slots(s)
         g_y.append(send(z_r.at[to_early], g_r.at[y, pl.ds(0, 128)], at_y(s)))
         g_y.append(send(z_r.at[to_late], g_r.at[y, pl.ds(128, 128)], at_y(s)))
+    for i in range(4):
+        rows = pl.ds(i * 256, 256)
+        dpre[rows, 256:384] = (dg_t[:, rows] * slope_gt[:, rows]).astype(BF16).T
+
     for kt in range(4):
         for qt in range(kt, 4):
             attend_back(a, kt, qt, BASE[kt] + qt - kt, dkv_own)

time: 74.4 us -> 74.4 us (level)
  no operation moved by 1% of the time
where the time goes in v4:
time: 74.4 us; the launch traced here: 74.2 us
  Pallas kernels  73.6 us (99%)
    pallas_call x1, Pallas kernels, body(): pl.pallas_call(kernel, name='hstu', out_shape=outs, in_specs=[vmem, pl.Bl...  71.7 us
    pallas_call x1, Pallas kernels, body(): pl.pallas_call(move, name='move', out_shape=outs, in_specs=[vmem] * 4, ou...  1.92 us

profile of v4, /device:TPU:4, one launch (start us, length us, event | category | flops | bytes accessed | tf_op | source)
XLA Modules:
  0.0 74.2 jit_solution(16164859784428179462)
XLA Ops:
  0.6 71.7 %hstu.1 = (bf16[256,512]{1,0:T(8,128)(2,1)}, bf16[256,512]{1,0:T(8,128)(2,1)}, f32[16,2048]{1,0:T(8,128)}, f32[16,512]{1,0:T(8,128)}) custom-call(bf16[256,512]{1,0:T(8,128)(2,1)} %tok.1, s32[1,2]{1,0:T(1,128)} %seq.1, bf16[16,2048]{1,0:T(8,128)(2,1)} %win.1, bf16[16,512]{1,0:T(8,128)(2,1)} %wout.1, bf16[256,512]{1,0:T(8,128)(2,1)} %cot.1), custom_call_target="tpu_custom_call" | custom-call | tf_op jit(solution)/shard_map/hstu/pallas_call | solution.py:614
  72.3 1.9 %move.1 = (bf16[256,512]{1,0:T(8,128)(2,1)}, bf16[256,512]{1,0:T(8,128)(2,1)}, f32[16,2048]{1,0:T(8,128)}, f32[16,512]{1,0:T(8,128)}) custom-call(bf16[256,512]{1,0:T(8,128)(2,1)} %get-tuple-element.8.refs_0_, bf16[256,512]{1,0:T(8,128)(2,1)} %get-tuple-element.9.refs_1_, f32[16,2048]{1,0:T(8,128)} %get-tuple-element.10.refs_2_, ...), custom_call_target="tpu_custom_call" | custom-call | tf_op jit(solution)/shard_map/move/pallas_call | solution.py:626
